TPU v7x, 32 devices: a whole 2x2x4 slice. The times are simulated.
32 devices in a mesh: snap: 2 (over y), gx: 16 (over z, x, core).
Axes of the slice: x: 2, y: 2, z: 4, core: 2. Of those that a mesh axis runs over, the one named last changes fastest.
Arguments:
- positions: float32 [1024, 3, 512], P(('snap', 'gx')), parts along dimension 0, may hold values from 0 to 16
- velocity: float32 [1024, 3, 512], P(('snap', 'gx')), parts along dimension 0, may hold values from -6 to 6
- counts: int32 [1024], P(('snap', 'gx')), parts along dimension 0, may hold values from 1 to 512, 131072 in all
- tile_ids: int32 [1024], P(('snap', 'gx')), parts along dimension 0, may hold values from 0 to 511, as said below
Outputs:
- level_fine: float32 [4, 512, 32, 256], P(None, ('snap', 'gx')), parts along dimension 1
- level_mid: float32 [4, 256, 2048], P(None, ('snap', 'gx')), parts along dimension 1
- level_coarse: float32 [4, 128, 512], P(None, ('snap', 'gx')), parts along dimension 1
There are 2 independent parts, one for each index of `snap`. A program takes and returns all parts, laid end to end along the dimension named above; each array names one. Nothing has to cross between parts.
Inputs may be any that keep to these rules, and one draw needn't show every extreme that they name: `tile_ids`: every tile id occurs once. The tile with id t is deposited into slab t // 32; one device holds at most 2 tiles of one slab, and exactly 2 of every slab it holds tiles of.
All inputs are finite; a program needn't handle non-finite values. No bound on the sum of `counts` on one device may be relied on, other than what follows from the above.
Results may differ from a plain program's by a relative error of at most 0.0021.
Values sent between devices are 32-bit elements; how exact they have to be, the bound alone decides.
No kernel may reach another device: no remote copies, remote signals or barrier semaphores. Data moves between devices by JAX's collectives and lax.ppermute only.
A program may use at most 128 MiB of HBM per device.

v0:
```python
import math

import jax
import jax.numpy as jnp
from jax import lax
from jax.sharding import PartitionSpec as P

TILE = 16
NY = 32
NZ = 256


MASS_UNIT = 4.0


def passed_along(shard, axis, by):
    devices = lax.axis_size(axis)
    return lax.ppermute(shard, axis, [(i, (i + by) % devices) for i in range(devices)])


def padded_2(block, sides, width):
    for axis, dim in sides:
        count = lax.axis_size(axis)
        forward = [(i, i + 1) for i in range(count - 1)]
        forward.append((count - 1, 0))
        backward = [(target, source) for source, target in forward]
        low = lax.ppermute(
            lax.slice_in_dim(block, block.shape[dim] - width, None, axis=dim), axis, forward
        )
        high = lax.ppermute(lax.slice_in_dim(block, 0, width, axis=dim), axis, backward)
        block = jnp.concatenate([low, block, high], axis=dim)
    return block


def smooth(far_low, near_low, centre, near_high, far_high):
    return (far_low + far_high + 4.0 * (near_low + near_high) + 6.0 * centre) * 0.0625


def smooth_along(field, axis):
    return smooth(
        jnp.roll(field, 2, axis),
        jnp.roll(field, 1, axis),
        field,
        jnp.roll(field, -1, axis),
        jnp.roll(field, -2, axis),
    )


def smooth_padded(padded):
    return smooth(padded[:, 0:-4], padded[:, 1:-3], padded[:, 2:-2], padded[:, 3:-1], padded[:, 4:])


def deposit_block(payload):
    rim_cells = TILE + 1
    block_size = payload.shape[0]
    capacity = payload.shape[2]
    lattice = jnp.arange(rim_cells, dtype=jnp.float32)
    spots = payload[:, 0:3]
    cell_floor = jnp.minimum(jnp.floor(spots), TILE - 1.0)
    fraction = spots - cell_floor
    weights = (lattice == cell_floor[..., None]).astype(jnp.float32) * (1.0 - fraction)[
        ..., None
    ] + (lattice == cell_floor[..., None] + 1.0).astype(jnp.float32) * fraction[..., None]
    planar = (
        (weights[:, 0, :, :, None] * weights[:, 1, :, None, :])
        .reshape(block_size, capacity, rim_cells * rim_cells)
        .astype(jnp.bfloat16)
    )
    charge = MASS_UNIT * jnp.concatenate([jnp.ones_like(payload[:, 3:4]), payload[:, 3:6]], axis=1)
    depth_rows = (
        (charge[:, :, :, None] * weights[:, 2, None, :, :])
        .transpose(0, 2, 1, 3)
        .reshape(block_size, capacity, 4 * rim_cells)
        .astype(jnp.bfloat16)
    )
    return jnp.einsum("npa,npb->nab", depth_rows, planar, preferred_element_type=jnp.float32)


def deposit_tiles(payload):
    count = payload.shape[0]
    block_size = math.gcd(count, 8)
    blocked = payload.reshape((count // block_size, block_size) + payload.shape[1:])
    result = lax.map(deposit_block, blocked)
    return result.reshape((count,) + result.shape[2:])


def assemble(tile_cells):
    rim_cells = TILE + 1
    rows_y = NY // TILE
    rows_z = NZ // TILE
    arranged = tile_cells.reshape(rows_y, rows_z, 4, rim_cells, rim_cells, rim_cells)
    arranged = arranged.transpose(2, 4, 0, 5, 1, 3)
    interior = arranged[..., :TILE]
    overflow = arranged[..., TILE]
    interior = jnp.concatenate(
        [interior[..., :1] + jnp.roll(overflow, 1, axis=4)[..., None], interior[..., 1:]], axis=5
    )
    overflow = interior[:, :, :, TILE]
    interior = interior[:, :, :, :TILE]
    interior = jnp.concatenate(
        [
            interior[:, :, :, :1] + jnp.roll(overflow, 1, axis=2)[:, :, :, None],
            interior[:, :, :, 1:],
        ],
        axis=3,
    )
    return interior.reshape(4, rim_cells, NY, NZ)


def compact(arrived, arrived_ids, held_tiles):
    tags = arrived_ids.astype(jnp.int32)
    local_index = jnp.where(tags >= 0, tags % held_tiles, held_tiles)
    empty = jnp.zeros((held_tiles,) + arrived.shape[1:], jnp.float32)
    return empty.at[local_index].set(arrived, mode="drop")


def halve_field(padded_field):
    halved = smooth_padded(padded_field)[:, ::2]
    halved = smooth_along(halved, 2)[:, :, ::2]
    return smooth_along(halved, 3)[:, :, :, ::2]


def on_device(positions, velocity, counts, tile_ids):
    held_tiles = positions.shape[0]
    capacity = positions.shape[2]
    devices = lax.axis_size("gx")
    per_peer = max(1, held_tiles // devices)
    alive_mask = jnp.arange(capacity, dtype=jnp.int32)[None, :] < counts[:, None]
    placed = jnp.where(alive_mask[:, None, :], positions, -2.0 * TILE)
    payload = jnp.concatenate([placed, velocity], axis=1)
    owners = tile_ids // held_tiles
    slot_order = jnp.arange(held_tiles, dtype=jnp.int32)
    earlier = (owners[:, None] == owners[None, :]) & (slot_order[None, :] < slot_order[:, None])
    bucket_rank = jnp.sum(earlier.astype(jnp.int32), axis=1)
    bucket_slot = owners * per_peer + bucket_rank
    outgoing_ids = (
        jnp.full((devices * per_peer,), -1.0, jnp.float32)
        .at[bucket_slot]
        .set(tile_ids.astype(jnp.float32))
    )
    outgoing = (
        jnp.zeros((devices * per_peer,) + payload.shape[1:], jnp.float32)
        .at[bucket_slot]
        .set(payload)
    )
    arrived, arrived_ids = (
        lax.all_to_all(outgoing, "gx", split_axis=0, concat_axis=0, tiled=True),
        lax.all_to_all(outgoing_ids, "gx", split_axis=0, concat_axis=0, tiled=True),
    )
    tile_cells = deposit_tiles(compact(arrived, arrived_ids, held_tiles))
    extended = assemble(tile_cells)
    deposit_raw = extended[:, :TILE]
    overflow = extended[:, TILE : TILE + 1]
    rim_width = 2
    arrived_plane = passed_along(overflow, "gx", 1)
    deposit = jnp.concatenate([deposit_raw[:, 0:1] + arrived_plane, deposit_raw[:, 1:]], axis=1)
    padded = padded_2(deposit, (("gx", 1),), rim_width)
    level_fine = smooth_along(smooth_along(smooth_padded(padded), 2), 3)
    padded_fine = padded_2(level_fine, (("gx", 1),), 2)
    level_mid = halve_field(padded_fine)
    padded_mid = padded_2(level_mid, (("gx", 1),), 2)
    level_coarse = halve_field(padded_mid)
    mid_shape = level_mid.shape
    coarse_shape = level_coarse.shape
    return (
        level_fine,
        level_mid.reshape(4, mid_shape[1], mid_shape[2] * mid_shape[3]),
        level_coarse.reshape(4, coarse_shape[1], coarse_shape[2] * coarse_shape[3]),
    )


def solution(mesh):
    placed = (
        P(("snap", "gx"), None, None),
        P(("snap", "gx"), None, None),
        P(("snap", "gx")),
        P(("snap", "gx")),
    )
    return jax.shard_map(
        on_device,
        mesh=mesh,
        in_specs=placed,
        out_specs=(
            P(None, ("snap", "gx"), None, None),
            P(None, ("snap", "gx"), None),
            P(None, ("snap", "gx"), None),
        ),
        check_vma=False,
    )
```

profile of v0, /device:TPU:1, one launch (start us, length us, event | category | flops | bytes accessed | tf_op | source)
XLA Modules:
  0.0 259.1 jit_solution(1160607137439876283)
XLA Ops:
  0.6 0.7 fusion.92
  1.6 0.7 scatter_custom_fusion
  2.2 0.7 all_to_all.9
  2.9 7.3 %all-to-all-start = ((f32[16,2,1]{1,2,0:T(1,128)}), f32[16,2,1]{1,2,0:T(1,128)S(1)}, u32[]{:S(2)}, u32[]{:S(2)}) async-start(f32[16,2,1]{1,2,0:T(1,128)} %bitcast.8), calls=%async_computation | async-start | bytes 16384 | tf_op jit(solution)/shard_map/all_to_all | solution.py:148
  10.3 0.7 iota_compare_fusion.3
  11.0 0.9 broadcast_select_fusion
  11.9 1.0 pad_maximum_fusion.5
  12.9 0.2 copy.49
  13.2 0.9 broadcast.129.clone
  14.0 4.4 %scatter_fusion = f32[32,6,512]{2,1,0:T(8,128)} fusion(f32[32,6,512]{2,1,0:T(8,128)} %broadcast.129.clone, s32[32]{0:T(128)S(1)} %compare_select_fusion.1, f32[32,6,512]{2,1,0:T(8,128)S(1)} %copy.49), kind=kCustom, calls=%fused_computation.1 | custom fusion | bytes 1179776 | tf_op jit(solution)/shard_map/scatter | solution.py:144
  18.4 6.0 %all-to-all-start.1 = ((f32[32,6,512]{2,1,0:T(8,128)}), f32[32,6,512]{2,1,0:T(8,128)S(1)}, u32[]{:S(2)}, u32[]{:S(2)}) async-start(f32[32,6,512]{2,1,0:T(8,128)} %scatter_fusion), calls=%async_computation.1 | async-start | bytes 1048576 | tf_op jit(solution)/shard_map/all_to_all | solution.py:147
  24.5 13.9 %all-to-all-done.1 = f32[32,6,512]{2,1,0:T(8,128)S(1)} async-done(((f32[32,6,512]{2,1,0:T(8,128)}), f32[32,6,512]{2,1,0:T(8,128)S(1)}, u32[]{:S(2)}, u32[]{:S(2)}) %all-to-all-start.1) | async-done | bytes 393248 | tf_op jit(solution)/shard_map/all_to_all | solution.py:147
  38.5 1.5 scatter_fusion.1
  40.3 14.0 %while.10 = (s32[]{:T(128)}, f32[4,8,68,289]{3,2,1,0:T(8,128)}, f32[4,8,6,512]{3,1,2,0:T(8,128)S(1)}, s32[]{:T(128)}) while((s32[]{:T(128)}, f32[4,8,68,289]{3,2,1,0:T(8,128)}, f32[4,8,6,512]{3,1,2,0:T(8,128)S(1)}, s32[]{:T(128)}) %tuple.67), condition=%wide.region_5.6_spmd, body=%wide.region_4.5_spmd.sunk | while | flops 165036032 | bytes 10994233 | solution.py:83
  40.6 0.5 multiply_convert_fusion.4
  41.2 2.7 %fusion.100 = f32[4,8,68,289]{3,2,1,0:T(8,128)} fusion(f32[4,8,68,289]{3,2,1,0:T(8,128)} %get-tuple-element.149, s32[]{:T(128)} %get-tuple-element.148, bf16[8,512,289]{1,0,2:T(8,128)(2,1)S(1)} %bitcast.60, bf16[8,512,68]{1,0,2:T(8,128)(2,1)S(1)} %bitcast.61), kind=kOutput, calls=%fused_computation.7.clone.1 | convolution fusion | flops 160989184 | bytes 3809792 | tf_op jit(solution)/shard_map/while/body/eval_jaxpr/npa,npb->nab/dot_general | solution.py:76
  44.1 0.5 multiply_convert_fusion.4
  44.6 2.6 %fusion.100 = f32[4,8,68,289]{3,2,1,0:T(8,128)} fusion(f32[4,8,68,289]{3,2,1,0:T(8,128)} %get-tuple-element.149, s32[]{:T(128)} %get-tuple-element.148, bf16[8,512,289]{1,0,2:T(8,128)(2,1)S(1)} %bitcast.60, bf16[8,512,68]{1,0,2:T(8,128)(2,1)S(1)} %bitcast.61), kind=kOutput, calls=%fused_computation.7.clone.1 | convolution fusion | flops 160989184 | bytes 3809792 | tf_op jit(solution)/shard_map/while/body/eval_jaxpr/npa,npb->nab/dot_general | solution.py:76
  47.5 0.5 multiply_convert_fusion.4
  48.1 2.7 %fusion.100 = f32[4,8,68,289]{3,2,1,0:T(8,128)} fusion(f32[4,8,68,289]{3,2,1,0:T(8,128)} %get-tuple-element.149, s32[]{:T(128)} %get-tuple-element.148, bf16[8,512,289]{1,0,2:T(8,128)(2,1)S(1)} %bitcast.60, bf16[8,512,68]{1,0,2:T(8,128)(2,1)S(1)} %bitcast.61), kind=kOutput, calls=%fused_computation.7.clone.1 | convolution fusion | flops 160989184 | bytes 3809792 | tf_op jit(solution)/shard_map/while/body/eval_jaxpr/npa,npb->nab/dot_general | solution.py:76
  51.0 0.5 multiply_convert_fusion.4
  51.6 2.7 %fusion.100 = f32[4,8,68,289]{3,2,1,0:T(8,128)} fusion(f32[4,8,68,289]{3,2,1,0:T(8,128)} %get-tuple-element.149, s32[]{:T(128)} %get-tuple-element.148, bf16[8,512,289]{1,0,2:T(8,128)(2,1)S(1)} %bitcast.60, bf16[8,512,68]{1,0,2:T(8,128)(2,1)S(1)} %bitcast.61), kind=kOutput, calls=%fused_computation.7.clone.1 | convolution fusion | flops 160989184 | bytes 3809792 | tf_op jit(solution)/shard_map/while/body/eval_jaxpr/npa,npb->nab/dot_general | solution.py:76
  54.3 5.6 %copy.51 = f32[4,8,68,289]{2,1,0,3:T(8,128)} copy(f32[4,8,68,289]{3,2,1,0:T(8,128)} %get-tuple-element.20) | data formatting | bytes 5030912 | tf_op jit(solution)/shard_map/while | solution.py:83
  59.9 14.2 %reshape_reshape.3 = f32[2,16,4,17,17,17]{3,2,1,0,5,4:T(4,128)} reshape(f32[4,8,68,289]{2,1,0,3:T(8,128)} %copy.51) | data formatting | bytes 5030912 | tf_op jit(solution)/shard_map/reshape;reshape | solution.py:91
  74.1 21.0 %slice.435 = f32[4,17,2,17,16,1]{5,0,4,2,3,1:T(4,128)} slice(f32[4,17,2,17,16,17]{5,0,4,2,3,1:T(4,128)} %bitcast.57), slice={[0:4], [0:17], [0:2], [0:17], [0:16], [16:17]} | slice | bytes 295936 | tf_op jit(solution)/shard_map/slice | solution.py:94
  95.1 12.7 %slice.438 = f32[4,17,2,17,16,15]{5,0,4,2,3,1:T(4,128)} slice(f32[4,17,2,17,16,17]{5,0,4,2,3,1:T(4,128)S(1)} %bitcast.59), slice={[0:4], [0:17], [0:2], [0:17], [0:16], [1:16]} | slice | bytes 4439040 | tf_op jit(solution)/shard_map/slice | solution.py:96
  107.8 19.2 %copy.52 = f32[4,17,2,17,16,1]{3,4,5,2,1,0:T(8,128)S(1)} copy(f32[4,17,2,17,16,1]{5,0,4,2,3,1:T(4,128)} %slice.435) | data formatting | bytes 295936 | tf_op jit(solution)/shard_map/slice | solution.py:94
  127.3 19.7 %copy.53 = f32[4,17,2,17,16,1]{5,0,4,2,3,1:T(4,128)} copy(f32[4,17,2,17,16,1]{3,4,5,2,1,0:T(8,128)S(1)} %maximum_bitcast_fusion.1) | data formatting | bytes 295936 | tf_op jit(solution)/shard_map/broadcast_in_dim | solution.py:96
  146.9 17.7 %slice_add_fusion = f32[4,17,2,17,16,1]{5,0,4,2,3,1:T(4,128)S(1)} fusion(f32[4,17,2,17,16,1]{5,0,4,2,3,1:T(4,128)} %copy.53, f32[4,17,2,17,16,17]{5,0,4,2,3,1:T(4,128)} %bitcast.58), kind=kLoop, calls=%fused_computation.22 | loop fusion | flops 36992 | bytes 443904 | tf_op jit(solution)/shard_map/add | solution.py:96
  164.7 2.0 maximum_bitcast_fusion
  166.9 0.3 slice-done.3
  167.2 0.7 slice-done.4
  167.9 1.8 maximum_add_fusion.4
  169.6 13.6 %fusion.9 = f32[4,17,2,16,16,16]{5,0,4,2,3,1:T(4,128)} fusion(f32[4,17,2,17,16,15]{5,0,4,2,3,1:T(4,128)S(1)} %bitcast.56, f32[4,17,2,17,16,1]{5,0,4,2,3,1:T(4,128)S(1)} %slice_add_fusion, f32[4,17,2,1,16,16]{5,0,4,2,3,1:T(4,128)} %maximum_add_fusion.4), kind=kLoop, calls=%fused_computation.24 | loop fusion | flops 2785280 | bytes 4734976 | tf_op jit(solution)/shard_map/concatenate | solution.py:100
  183.2 13.4 %copy.55 = f32[4,17,2,16,16,16]{5,4,3,2,1,0:T(8,128)} copy(f32[4,17,2,16,16,16]{5,0,4,2,3,1:T(4,128)} %fusion.9) | data formatting | bytes 4456448 | tf_op jit(solution)/shard_map/concatenate | solution.py:100
  196.6 12.0 %reshape.117 = f32[4,17,32,256]{3,2,1,0:T(8,128)S(1)} reshape(f32[4,17,2,16,16,16]{5,4,3,2,1,0:T(8,128)} %copy.55) | data formatting | bytes 4456448 | tf_op jit(solution)/shard_map/reshape | solution.py:107
  208.5 0.5 collective-permute-start.1
  209.3 0.8 collective-permute-start
  210.1 1.0 collective-permute-done.1
  211.1 5.3 %collective-permute-start.2 = (f32[4,2,32,256]{3,2,1,0:T(8,128)S(1)}, f32[4,2,32,256]{3,2,1,0:T(8,128)S(1)}, u32[]{:S(2)}, u32[]{:S(2)}) collective-permute-start(f32[4,2,32,256]{3,2,1,0:T(8,128)S(1)} %fusion.45), channel_id=1, source_target_pairs={{1,0},{2,1},{3,2},{4,3},{5,4},{6,5},{7,6},{8,7},{9,8},{10,9},{11,1... | collective-permute-start | bytes 786440 | tf_op jit(solution)/shard_map/ppermute | solution.py:30
  216.4 0.3 pad_maximum_fusion.1
  216.7 4.5 %collective-permute-done.2 = f32[4,2,32,256]{3,2,1,0:T(8,128)S(1)} collective-permute-done((f32[4,2,32,256]{3,2,1,0:T(8,128)S(1)}, f32[4,2,32,256]{3,2,1,0:T(8,128)S(1)}, u32[]{:S(2)}, u32[]{:S(2)}) %collective-permute-start.2) | collective-permute-done | bytes 262176 | tf_op jit(solution)/shard_map/ppermute | solution.py:30
  221.1 1.3 broadcast_multiply_fusion.2
  222.5 0.5 fusion.71
  223.0 0.5 fusion.73
  223.7 1.8 broadcast_multiply_fusion.1
  225.6 0.8 fusion.67
  226.4 0.8 fusion.69
  227.2 0.4 fusion.66
  227.6 0.4 fusion.68
  228.0 2.2 broadcast_multiply_fusion
  230.3 0.5 collective-permute-start.4
  230.8 5.6 %collective-permute-done.3 = f32[4,2,32,256]{3,2,1,0:T(8,128)S(1)} collective-permute-done((f32[4,2,32,256]{3,2,1,0:T(8,128)S(1)}, f32[4,2,32,256]{3,2,1,0:T(8,128)S(1)}, u32[]{:S(2)}, u32[]{:S(2)}) %collective-permute-start.3) | collective-permute-done | bytes 262176 | tf_op jit(solution)/shard_map/ppermute | solution.py:27
  236.4 2.5 collective-permute-done.4
  239.0 1.2 fusion.18
  240.8 0.7 fusion.33
  241.5 0.3 slice.394
  242.5 0.5 fusion.37
  243.0 8.9 %slice.403 = f32[4,8,16,128]{3,2,1,0:T(8,128)S(1)} slice(f32[4,8,16,256]{3,2,1,0:T(8,128)S(1)} %fusion.37), slice={[0:4:1], [0:8:1], [0:16:1], [0:256:2]} | slice | bytes 524288 | tf_op jit(solution)/shard_map/slice | solution.py:120
  252.0 0.5 collective-permute-start.6
  252.5 0.7 reshape.118
  253.4 2.7 %collective-permute-done.6 = f32[4,2,16,128]{3,2,1,0:T(8,128)S(1)} collective-permute-done((f32[4,2,16,128]{3,2,1,0:T(8,128)S(1)}, f32[4,2,16,128]{3,2,1,0:T(8,128)S(1)}, u32[]{:S(2)}, u32[]{:S(2)}) %collective-permute-start.6) | collective-permute-done | bytes 65568 | tf_op jit(solution)/shard_map/ppermute | solution.py:30
  257.0 1.4 slice.428
  258.4 0.7 reshape.119
  (84 shorter events, 5.0 us)
Async XLA Ops:
  2.9 15.4 %all-to-all-start = ((f32[16,2,1]{1,2,0:T(1,128)}), f32[16,2,1]{1,2,0:T(1,128)S(1)}, u32[]{:S(2)}, u32[]{:S(2)}) async-start(f32[16,2,1]{1,2,0:T(1,128)} %bitcast.8), calls=%async_computation | async-start | bytes 16384 | tf_op jit(solution)/shard_map/all_to_all | solution.py:148
  18.4 20.1 %all-to-all-start.1 = ((f32[32,6,512]{2,1,0:T(8,128)}), f32[32,6,512]{2,1,0:T(8,128)S(1)}, u32[]{:S(2)}, u32[]{:S(2)}) async-start(f32[32,6,512]{2,1,0:T(8,128)} %scatter_fusion), calls=%async_computation.1 | async-start | bytes 1048576 | tf_op jit(solution)/shard_map/all_to_all | solution.py:147
  74.1 21.0 %copy-start = (f32[2,16,4,17,17,17]{3,2,1,0,5,4:T(4,128)S(1)}, f32[2,16,4,17,17,17]{3,2,1,0,5,4:T(4,128)}, u32[]{:S(2)}) copy-start(f32[2,16,4,17,17,17]{3,2,1,0,5,4:T(4,128)} %reshape_reshape.3) | copy-start | bytes 7546372
  146.9 19.9 %slice-start = ((s8[18939904]{0:T(1024)(128)(4,1)}), s8[4194304]{0:T(1024)(128)(4,1)S(1)}, s32[]{:S(2)}) async-start(s8[18939904]{0:T(1024)(128)(4,1)} %bitcast.55), calls=%async_computation.2 | async-start | bytes 8388608
  146.9 19.9 %slice-start.1 = ((s8[18939904]{0:T(1024)(128)(4,1)}), s8[4194304]{0:T(1024)(128)(4,1)S(1)}, s32[]{:S(2)}) async-start(s8[18939904]{0:T(1024)(128)(4,1)} %bitcast.55), calls=%async_computation.3 | async-start | bytes 8388608
  146.9 19.9 %slice-start.2 = ((s8[18939904]{0:T(1024)(128)(4,1)}), s8[4194304]{0:T(1024)(128)(4,1)S(1)}, s32[]{:S(2)}) async-start(s8[18939904]{0:T(1024)(128)(4,1)} %bitcast.55), calls=%async_computation.4 | async-start | bytes 8388608
  164.6 2.5 slice-start.3
  164.6 3.2 %slice-start.4 = ((s8[18939904]{0:T(1024)(128)(4,1)}), s8[2162688]{0:T(1024)(128)(4,1)S(1)}, s32[]{:S(2)}) async-start(s8[18939904]{0:T(1024)(128)(4,1)} %bitcast.55), calls=%async_computation.6 | async-start | bytes 4325376
  208.5 2.5 collective-permute-start.1
  209.3 7.1 %collective-permute-start = (f32[4,2,32,256]{3,2,1,0:T(8,128)S(1)}, f32[4,2,32,256]{3,2,1,0:T(8,128)S(1)}, u32[]{:S(2)}, u32[]{:S(2)}) collective-permute-start(f32[4,2,32,256]{3,2,1,0:T(8,128)S(1)} %slice.441), channel_id=1, source_target_pairs={{0,1},{1,2},{2,3},{3,4},{4,5},{5,6},{6,7},{7,8},{8,9},{9,10},{10,1... | collective-permute-start | bytes 786440 | tf_op jit(solution)/shard_map/ppermute | solution.py:27
  211.1 10.0 %collective-permute-start.2 = (f32[4,2,32,256]{3,2,1,0:T(8,128)S(1)}, f32[4,2,32,256]{3,2,1,0:T(8,128)S(1)}, u32[]{:S(2)}, u32[]{:S(2)}) collective-permute-start(f32[4,2,32,256]{3,2,1,0:T(8,128)S(1)} %fusion.45), channel_id=1, source_target_pairs={{1,0},{2,1},{3,2},{4,3},{5,4},{6,5},{7,6},{8,7},{9,8},{10,9},{11,1... | collective-permute-start | bytes 786440 | tf_op jit(solution)/shard_map/ppermute | solution.py:30
  230.2 9.9 %copy-start.1 = (f32[4,16,32,256]{3,2,1,0:T(8,128)}, f32[4,16,32,256]{3,2,1,0:T(8,128)S(1)}, u32[]{:S(2)}) copy-start(f32[4,16,32,256]{3,2,1,0:T(8,128)S(1)} %get-tuple-element.39) | copy-start | bytes 6291460
  230.2 6.2 %collective-permute-start.3 = (f32[4,2,32,256]{3,2,1,0:T(8,128)S(1)}, f32[4,2,32,256]{3,2,1,0:T(8,128)S(1)}, u32[]{:S(2)}, u32[]{:S(2)}) collective-permute-start(f32[4,2,32,256]{3,2,1,0:T(8,128)S(1)} %get-tuple-element.53), channel_id=1, source_target_pairs={{0,1},{1,2},{2,3},{3,4},{4,5},{5,6},{6,7},{7,8},{8,9},{9,10},{10,1... | collective-permute-start | bytes 786440 | tf_op jit(solution)/shard_map/ppermute | solution.py:27
  230.3 8.7 %collective-permute-start.4 = (f32[4,2,32,256]{3,2,1,0:T(8,128)S(1)}, f32[4,2,32,256]{3,2,1,0:T(8,128)S(1)}, u32[]{:S(2)}, u32[]{:S(2)}) collective-permute-start(f32[4,2,32,256]{3,2,1,0:T(8,128)S(1)} %get-tuple-element.54), channel_id=1, source_target_pairs={{1,0},{2,1},{3,2},{4,3},{5,4},{6,5},{7,6},{8,7},{9,8},{10,9},{11,1... | collective-permute-start | bytes 786440 | tf_op jit(solution)/shard_map/ppermute | solution.py:30
  252.0 1.4 collective-permute-start.5
  252.0 4.0 %collective-permute-start.6 = (f32[4,2,16,128]{3,2,1,0:T(8,128)S(1)}, f32[4,2,16,128]{3,2,1,0:T(8,128)S(1)}, u32[]{:S(2)}, u32[]{:S(2)}) collective-permute-start(f32[4,2,16,128]{3,2,1,0:T(8,128)S(1)} %get-tuple-element.90), channel_id=1, source_target_pairs={{1,0},{2,1},{3,2},{4,3},{5,4},{6,5},{7,6},{8,7},{9,8},{10,9},{11,1... | collective-permute-start | bytes 196616 | tf_op jit(solution)/shard_map/ppermute | solution.py:30
where the time goes:
time: 262 us; the launch traced here: 259 us
  local copies, waits for them, and re-layouts  146 us (56%)
  other arithmetic  50.1 us (19%)
  waiting for transfers between devices  30.3 us (12%)
  starting transfers between devices  21.1 us (8%)
  matrix products  10.6 us (4%)
    slice x2, local copies, waits for them, and re-layouts, assemble(): overflow = arranged[..., TILE]  40.2 us
    broadcast_in_dim x1, local copies, waits for them, and re-layouts, assemble(): jnp.roll(overflow, 1, axis=4)[..., None]  19.7 us
    add x1, other arithmetic, assemble(): interior[..., :1] + jnp.roll(overflow, 1, axis=4)[..., None]  17.7 us
    another operation x1, local copies, waits for them, and re-layouts, assemble(): tile_cells.reshape(rows_y, rows_z, 4, rim_cells, rim_cells, rim_cells)  14.2 us
    all_to_all x1, waiting for transfers between devices, on_device(): lax.all_to_all(outgoing, 'gx', split_axis=0, concat_axis=0, tiled=True)  13.9 us
    concatenate x1, other arithmetic, assemble(): jnp.concatenate([interior[:, :, :, :1] + jnp.roll(overflow, 1, axis=2)[:,...  13.6 us
    concatenate x1, local copies, waits for them, and re-layouts, assemble(): jnp.concatenate([interior[:, :, :, :1] + jnp.roll(overflow, 1, axis=2)[:,...  13.4 us
    slice x1, local copies, waits for them, and re-layouts, assemble(): interior[..., 1:]  12.7 us
  transfers between devices with their start and end apart: 9, of which 7 were waited for; matrix products, arithmetic and copies ran while one was open for 4% of the time, Pallas kernels for 0%

commit v1 on v0

v1 whole, which is shorter than its diff:
```python
import functools
import math

import jax
import jax.numpy as jnp
import ml_dtypes
import numpy as np
from jax import lax
from jax.experimental import pallas as pl
from jax.experimental.pallas import tpu as pltpu
from jax.sharding import PartitionSpec as P

TILE = 16
NY = 32
NZ = 256
LANES = 128
QUAD = 4
PLANES = TILE + 1
ROWS = PLANES * NY
WIDTH = 4 * QUAD * TILE
QUADS = NZ // (QUAD * TILE)
MASS_UNIT = 4.0
DEAD = -32.0
Y_SHIFT = 2

RIGHT = 3
LEFT = 2


def taps(levels):
    row = np.array([1.0])
    for level in range(levels):
        once = np.array([1.0, 4.0, 6.0, 4.0, 1.0]) / 16.0
        spread = np.zeros(4 * max(1, 2 ** (level - 1)) + 1)
        spread[:: max(1, 2 ** (level - 1))] = once
        row = np.convolve(row, spread)
    return row


def periodic(levels, size):
    step = 2 ** (levels - 1)
    row = taps(levels)
    half = len(row) // 2
    out = np.zeros((size // step, size))
    for i in range(size // step):
        for k, value in enumerate(row):
            out[i, (i * step + k - half) % size] += value
    return out


def open_ended(levels, below, above):
    step = 2 ** (levels - 1)
    row = taps(levels)
    half = len(row) // 2
    count = TILE // step
    out = np.zeros((below + count + above, PLANES))
    for i in range(-below, count + above):
        for k, value in enumerate(row):
            plane = i * step + k - half
            if 0 <= plane < PLANES:
                out[i + below, plane] += value
    return out


def split_host(matrix):
    high = matrix.astype(ml_dtypes.bfloat16)
    low = (matrix - high.astype(np.float64)).astype(ml_dtypes.bfloat16)
    return high, low


def depth_matrix():
    fine = periodic(1, NZ).T / 256.0
    mid = periodic(2, NZ).T
    coarse_high, coarse_low = split_host(periodic(3, NZ).T)
    columns = np.concatenate(
        [
            fine,
            mid,
            coarse_high.astype(np.float64),
            coarse_low.astype(np.float64),
        ],
        axis=1,
    )
    swapped = columns[np.arange(NZ) ^ (QUAD * TILE)]
    both = np.stack([columns, swapped])
    return np.concatenate([both, both], axis=1).astype(ml_dtypes.bfloat16)


def plane_matrix():
    rolled = (np.arange(NY) + Y_SHIFT) % NY
    mid_y = periodic(2, NY)[:, rolled]
    coarse_y = periodic(3, NY)[:, rolled]
    mid_x = open_ended(2, LEFT, RIGHT)
    coarse_x = open_ended(3, LEFT, RIGHT)
    rows = []
    for y in range(NY // 2):
        for m in range(TILE // 2):
            rows.append(np.kron(mid_x[LEFT + m], mid_y[y]))
    for m in list(range(-LEFT, 0)) + list(range(TILE // 2, TILE // 2 + RIGHT)):
        for y in range(NY // 2):
            rows.append(np.kron(mid_x[LEFT + m], mid_y[y]))
    order = list(range(0, NY // 4, 2)) + list(range(1, NY // 4, 2))
    for y in order:
        for k in range(TILE // 4):
            rows.append(np.kron(coarse_x[LEFT + k], coarse_y[y]))
    for k in list(range(-LEFT, 0)) + list(range(TILE // 4, TILE // 4 + RIGHT)):
        for y in order:
            rows.append(np.kron(coarse_x[LEFT + k], coarse_y[y]))
    high, low = split_host(np.stack(rows))
    return np.concatenate([high, low], axis=1)


def split(value):
    high = value.astype(jnp.bfloat16)
    return high, (value - high.astype(jnp.float32)).astype(jnp.bfloat16)


def hat(position, lattice):
    return jnp.maximum(1.0 - jnp.abs(position - lattice), 0.0)


def bucket_kernel(per_peer, ids_ref, counts_ref, spots_ref, speed_ref, out_ref, filled_ref):
    _, held, capacity = spots_ref.shape
    devices = out_ref.shape[0]
    chunks = capacity // LANES
    size = 6 * chunks
    for owner in range(devices):
        filled_ref[owner] = 0
    if devices * per_peer > held:
        out_ref[:, per_peer * size :, :] = jnp.full((devices, 8, LANES), -1.0, jnp.float32)

    for tile in range(held):
        tag = ids_ref[tile]
        count = counts_ref[tile]
        owner = tag // held
        rank = filled_ref[owner]
        filled_ref[owner] = rank + 1
        base = pl.multiple_of(rank * size, 8)
        for chunk in range(chunks):
            cut = slice(chunk * LANES, (chunk + 1) * LANES)
            lane = lax.broadcasted_iota(jnp.int32, (1, LANES), 1) + chunk * LANES
            for a in range(3):
                spots = spots_ref[a, tile : tile + 1, cut]
                if a == 0:
                    spots = jnp.where(lane < count, spots, DEAD)
                out_ref[owner, pl.ds(base + 6 * chunk + a, 1), :] = spots
                speed = speed_ref[a, tile : tile + 1, cut]
                out_ref[owner, pl.ds(base + 6 * chunk + 3 + a, 1), :] = speed
        mark = jnp.full((1, LANES), (tag % held).astype(jnp.float32), jnp.float32)
        out_ref[owner, pl.ds(per_peer * size + rank, 1), :] = mark


def bucket(positions, velocity, counts, tile_ids, devices, per_peer):
    capacity = positions.shape[2]
    rows = per_peer * 6 * (capacity // LANES) + 8
    return pl.pallas_call(
        functools.partial(bucket_kernel, per_peer),
        out_shape=jax.ShapeDtypeStruct((devices, rows, LANES), jnp.float32),
        in_specs=[
            pl.BlockSpec(memory_space=pltpu.SMEM),
            pl.BlockSpec(memory_space=pltpu.SMEM),
            pl.BlockSpec(memory_space=pltpu.VMEM),
            pl.BlockSpec(memory_space=pltpu.VMEM),
        ],
        out_specs=pl.BlockSpec(memory_space=pltpu.VMEM),
        scratch_shapes=[pltpu.SMEM((devices,), jnp.int32)],
        compiler_params=pltpu.CompilerParams(vmem_limit_bytes=6 * 2**20),
        name="bucket",
    )(tile_ids, counts, positions.transpose(1, 0, 2), velocity.transpose(1, 0, 2))


def deposit_kernel(
    per_peer,
    chunks,
    arrived_ref,
    depth_ref,
    plane_ref,
    fine_ref,
    rim_ref,
    mid_ref,
    coarse_ref,
    right_ref,
    left_ref,
    slot_ref,
    marks_ref,
    planar_ref,
    sums_ref,
    spread_ref,
    rest_ref,
    inside_ref,
    sems,
):
    devices = arrived_ref.shape[0]
    size = 6 * chunks
    capacity = chunks * LANES
    marks = pltpu.make_async_copy(
        arrived_ref.at[:, per_peer * size : per_peer * size + 8], marks_ref, sems.at[4]
    )
    marks.start()
    marks.wait()

    def look(slot, carry):
        tag = marks_ref[slot // per_peer, slot % per_peer, 0].astype(jnp.int32)

        @pl.when(tag >= 0)
        def _():
            slot_ref[tag] = slot

        return carry

    lax.fori_loop(0, devices * per_peer, look, 0)

    def row_of(shape, dim):
        return lax.broadcasted_iota(jnp.int32, shape, dim)

    def tile_terms(q, parity, t, ty, buffer):
        local = ty * (NZ // TILE) + q * QUAD + t
        slot = slot_ref[local]
        device = slot // per_peer
        base = pl.multiple_of((slot % per_peer) * size, 8)
        y_lattice = ((row_of((NY, LANES), 0) + (Y_SHIFT + TILE * ty)) % NY).astype(jnp.float32)
        x_lattice = row_of((24, LANES), 0).astype(jnp.float32)
        z_lattice = row_of((TILE, LANES), 0).astype(jnp.float32)
        depth_chunks = []
        for chunk in range(chunks):

            def particle(a, rows):
                line = arrived_ref[device, pl.ds(base + (6 * chunk + a), 1), :]
                return jnp.broadcast_to(line, (rows, LANES))

            weights_x = hat(particle(0, 24), x_lattice)
            weights_y = hat(particle(1, NY), y_lattice)
            start = ty * capacity + chunk * LANES
            for x in range(PLANES):
                planar = jnp.broadcast_to(weights_x[x : x + 1], (NY, LANES)) * weights_y
                planar_ref[buffer, x * NY : (x + 1) * NY, start : start + LANES] = planar.astype(
                    jnp.bfloat16
                )
            weights_z = hat(particle(2, TILE), z_lattice)
            spot_z = particle(2, TILE)
            past = jnp.where(
                row_of((TILE, LANES), 0) == 0, jnp.maximum(spot_z - (TILE - 1.0), 0.0), 0.0
            )
            charges = [jnp.full((TILE, LANES), MASS_UNIT, jnp.float32)] + [
                MASS_UNIT * particle(a, TILE) for a in (3, 4, 5)
            ]
            zero = jnp.zeros((TILE, LANES), jnp.bfloat16)
            pieces = []
            for place in range(4):
                c = place ^ parity
                inside = (charges[c] * weights_z).astype(jnp.bfloat16)
                other = charges[c ^ 1] if t == QUAD - 1 else charges[c]
                outside = (other * past).astype(jnp.bfloat16)
                for block in range(QUAD):
                    if block == t:
                        pieces.append(inside)
                    elif block == (t + 1) % QUAD:
                        pieces.append(outside)
                    else:
                        pieces.append(zero)
            depth_chunks.append(jnp.concatenate(pieces, axis=0))
        return jnp.concatenate(depth_chunks, axis=1)

    def pair_of_quads(h, carry):
        for parity in range(2):
            q = 2 * h + parity
            for t in range(QUAD):
                buffer = t % 2
                depth = jnp.concatenate(
                    [tile_terms(q, parity, t, ty, buffer) for ty in range(NY // TILE)], axis=1
                )
                result = lax.dot_general(
                    planar_ref[buffer],
                    depth,
                    (((1,), (1,)), ((), ())),
                    preferred_element_type=jnp.float32,
                )
                if t == 0:
                    sums_ref[q, 0] = result
                elif t == QUAD - 1:
                    sums_ref[q, 1] = result
                else:
                    sums_ref[q, 0] = sums_ref[q, 0] + result
        return carry

    lax.fori_loop(0, QUADS // 2, pair_of_quads, 0)

    lane = row_of((NY, LANES), 1)
    first_half = lane < LANES // 2
    inner = (lane % (LANES // 2)) != 0

    def window(q, plane, half):
        rows = slice(plane * NY, (plane + 1) * NY)
        cut = slice(half * LANES, (half + 1) * LANES)
        before = (q - 1) % QUADS
        return sums_ref[q, 0, rows, cut] + jnp.where(
            inner, sums_ref[q, 1, rows, cut], sums_ref[before, 1, rows, cut]
        )

    for half in range(2):
        for plane in range(PLANES):
            rows = slice(plane * NY, (plane + 1) * NY)
            for h in range(2):
                even, odd = window(2 * h, plane, half), window(2 * h + 1, plane, half)
                for parity in range(2):
                    one, two = (even, odd) if parity == 0 else (odd, even)
                    high, low = split(jnp.where(first_half, one, two))
                    spread_ref[2 * half + parity, rows, h * LANES : (h + 1) * LANES] = high
                    spread_ref[2 * half + parity, rows, NZ + h * LANES : NZ + (h + 1) * LANES] = low

    def inside(c):
        return pltpu.make_async_copy(
            inside_ref.at[c], fine_ref.at[c, RIGHT : TILE - LEFT], sems.at[c]
        )

    def channel(c, carry):
        levels = jnp.dot(
            spread_ref[c], depth_ref[c % 2], preferred_element_type=jnp.float32
        )
        coarse = levels[:, 3 * LANES :]
        coarse = coarse + pltpu.roll(coarse, LANES // 2, 1)
        mid_high, mid_low = split(levels[:, 2 * LANES : 3 * LANES])
        coarse_high, coarse_low = split(coarse)
        rest_ref[0, :, :LANES] = mid_high
        rest_ref[0, :, LANES:] = coarse_high
        rest_ref[1, :, :LANES] = mid_low
        rest_ref[1, :, LANES:] = coarse_low

        zero = jnp.zeros((NY, NZ), jnp.float32)
        held = [zero] * 4
        for plane in range(-LEFT, TILE + RIGHT):
            source = plane + 2
            if source < PLANES:
                field = levels[source * NY : (source + 1) * NY, :NZ]
                lag = pltpu.roll(field, 2, 0)
                twice = field + lag
                value = twice + pltpu.roll(twice, 2, 0) + 4.0 * (pltpu.roll(twice, 1, 0) + lag)
            else:
                value = zero
            for k in range(4):
                following = value + held[k]
                held[k] = value
                value = following
            if plane < 0:
                row = (c * LEFT + plane + LEFT) * 2 * NY
                left_ref[pl.ds(pl.multiple_of(row, 8), NY), :] = value[:, :LANES]
                left_ref[pl.ds(pl.multiple_of(row + NY, 8), NY), :] = value[:, LANES:]
            elif plane >= TILE:
                row = (c * RIGHT + plane - TILE) * 2 * NY
                right_ref[pl.ds(pl.multiple_of(row, 8), NY), :] = value[:, :LANES]
                right_ref[pl.ds(pl.multiple_of(row + NY, 8), NY), :] = value[:, LANES:]
            elif plane < RIGHT:
                rim_ref[c, plane] = value
            elif plane >= TILE - LEFT:
                rim_ref[c, RIGHT + plane - (TILE - LEFT)] = value
            else:
                inside_ref[c, plane - RIGHT] = value

        inside(c).start()
        high_rows, low_rows = plane_ref[:, :ROWS], plane_ref[:, ROWS:]
        packed = (
            jnp.dot(high_rows, rest_ref[0], preferred_element_type=jnp.float32)
            + jnp.dot(high_rows, rest_ref[1], preferred_element_type=jnp.float32)
            + jnp.dot(low_rows, rest_ref[0], preferred_element_type=jnp.float32)
        )
        mid_rows = NY // 2 * (TILE // 2)
        mid_edge = NY // 2
        mid_ref[c] = packed[:mid_rows, :LANES]
        at = mid_rows
        row = 4 * LEFT * 2 * NY + c * LEFT * mid_edge
        left_ref[pl.ds(pl.multiple_of(row, 8), LEFT * mid_edge), :] = packed[
            at : at + LEFT * mid_edge, :LANES
        ]
        at += LEFT * mid_edge
        row = 4 * RIGHT * 2 * NY + c * RIGHT * mid_edge
        right_ref[pl.ds(pl.multiple_of(row, 8), RIGHT * mid_edge), :] = packed[
            at : at + RIGHT * mid_edge, :LANES
        ]
        at += RIGHT * mid_edge
        coarse_rows = NY // 4 * (TILE // 4)
        coarse_edge = NY // 4
        coarse_ref[c] = packed[at : at + coarse_rows, LANES:]
        at += coarse_rows
        row = 4 * LEFT * (2 * NY + mid_edge) + c * LEFT * coarse_edge
        left_ref[pl.ds(pl.multiple_of(row, 8), LEFT * coarse_edge), :] = packed[
            at : at + LEFT * coarse_edge, LANES:
        ]
        at += LEFT * coarse_edge
        row = 4 * RIGHT * (2 * NY + mid_edge) + c * RIGHT * coarse_edge
        right_ref[pl.ds(pl.multiple_of(row, 8), RIGHT * coarse_edge), :] = packed[
            at : at + RIGHT * coarse_edge, LANES:
        ]
        return carry

    lax.fori_loop(0, 4, channel, 0)
    for c in range(4):
        inside(c).wait()


def edge_rows(planes):
    return 4 * planes * (2 * NY + NY // 2 + NY // 4)


def deposit(arrived, per_peer, capacity):
    devices = arrived.shape[0]
    f32 = jnp.float32
    vmem = pl.BlockSpec(memory_space=pltpu.VMEM)
    return pl.pallas_call(
        functools.partial(deposit_kernel, per_peer, capacity // LANES),
        out_shape=[
            jax.ShapeDtypeStruct((4, TILE, NY, NZ), f32),
            jax.ShapeDtypeStruct((4, RIGHT + LEFT, NY, NZ), f32),
            jax.ShapeDtypeStruct((4, NY // 2 * (TILE // 2), LANES), f32),
            jax.ShapeDtypeStruct((4, NY // 4 * (TILE // 4), LANES), f32),
            jax.ShapeDtypeStruct((edge_rows(RIGHT), LANES), f32),
            jax.ShapeDtypeStruct((edge_rows(LEFT), LANES), f32),
        ],
        in_specs=[vmem] * 3,
        out_specs=[pl.BlockSpec(memory_space=pl.ANY)] + [vmem] * 5,
        scratch_shapes=[
            pltpu.SMEM((NY // TILE * (NZ // TILE),), jnp.int32),
            pltpu.SMEM((devices, 8, LANES), f32),
            pltpu.VMEM((2, ROWS, NY // TILE * capacity), jnp.bfloat16),
            pltpu.VMEM((QUADS, 2, ROWS, WIDTH), f32),
            pltpu.VMEM((4, ROWS, 2 * NZ), jnp.bfloat16),
            pltpu.VMEM((2, ROWS, 2 * LANES), jnp.bfloat16),
            pltpu.VMEM((4, TILE - RIGHT - LEFT, NY, NZ), f32),
            pltpu.SemaphoreType.DMA((5,)),
        ],
        compiler_params=pltpu.CompilerParams(vmem_limit_bytes=28 * 2**20),
        name="deposit",
    )(arrived, jnp.asarray(depth_matrix()), jnp.asarray(plane_matrix()))


def join_kernel(
    inside_ref, rim_ref, mid_in_ref, coarse_in_ref, low_ref, high_ref,
    fine_ref, mid_ref, coarse_ref, edge_ref, mid_sum, coarse_sum, sems,
):
    for c in range(4):
        for plane in range(RIGHT):
            row = (c * RIGHT + plane) * 2 * NY
            edge_ref[c, plane, :, :LANES] = rim_ref[c, plane, :, :LANES] + low_ref[row : row + NY]
            edge_ref[c, plane, :, LANES:] = (
                rim_ref[c, plane, :, LANES:] + low_ref[row + NY : row + 2 * NY]
            )
        for plane in range(LEFT):
            row = (c * LEFT + plane) * 2 * NY
            at = RIGHT + plane
            edge_ref[c, at, :, :LANES] = rim_ref[c, at, :, :LANES] + high_ref[row : row + NY]
            edge_ref[c, at, :, LANES:] = (
                rim_ref[c, at, :, LANES:] + high_ref[row + NY : row + 2 * NY]
            )
    first = pltpu.make_async_copy(edge_ref.at[:, :RIGHT], fine_ref.at[:, :RIGHT], sems.at[1])
    last = pltpu.make_async_copy(edge_ref.at[:, RIGHT:], fine_ref.at[:, TILE - LEFT :], sems.at[0])
    first.start()
    last.start()
    mid_sum[...] = mid_in_ref[...]
    coarse_sum[...] = coarse_in_ref[...]
    for sent, planes, first_of in ((low_ref, RIGHT, False), (high_ref, LEFT, True)):
        for c in range(4):
            for i in range(planes):
                count, edge = TILE // 2, NY // 2
                m = count - planes + i if first_of else i
                row = 4 * planes * 2 * NY + (c * planes + i) * edge
                where = pl.ds(m, edge, stride=count)
                mid_sum[c, where, :] = mid_sum[c, where, :] + sent[row : row + edge]
                count, edge = TILE // 4, NY // 4
                k = count - planes + i if first_of else i
                row = 4 * planes * (2 * NY + NY // 2) + (c * planes + i) * edge
                where = pl.ds(k, edge, stride=count)
                coarse_sum[c, where, :] = coarse_sum[c, where, :] + sent[row : row + edge]
    for c in range(4):
        for y in range(NY // 2):
            rows = TILE // 2
            mid_ref[c, :, y * LANES : (y + 1) * LANES] = mid_sum[c, y * rows : (y + 1) * rows]
        for pair in range(NY // 8):
            rows = TILE // 4
            even = coarse_sum[c, pair * rows : (pair + 1) * rows]
            at = NY // 8 * rows + pair * rows
            odd = coarse_sum[c, at : at + rows]
            lane = lax.broadcasted_iota(jnp.int32, even.shape, 1)
            coarse_ref[c, :, pair * LANES : (pair + 1) * LANES] = jnp.where(
                lane < LANES // 2, even, odd
            )
    first.wait()
    last.wait()


def join(inside, rim, mid, coarse, from_low, from_high):
    f32 = jnp.float32
    vmem = pl.BlockSpec(memory_space=pltpu.VMEM)
    far = pl.BlockSpec(memory_space=pl.ANY)
    return pl.pallas_call(
        join_kernel,
        out_shape=[
            jax.ShapeDtypeStruct((4, TILE, NY, NZ), f32),
            jax.ShapeDtypeStruct((4, TILE // 2, NY // 2 * (NZ // 2)), f32),
            jax.ShapeDtypeStruct((4, TILE // 4, NY // 4 * (NZ // 4)), f32),
        ],
        in_specs=[far] + [vmem] * 5,
        out_specs=[far, vmem, vmem],
        scratch_shapes=[
            pltpu.VMEM((4, RIGHT + LEFT, NY, NZ), f32),
            pltpu.VMEM(mid.shape, f32),
            pltpu.VMEM(coarse.shape, f32),
            pltpu.SemaphoreType.DMA((2,)),
        ],
        input_output_aliases={0: 0},
        compiler_params=pltpu.CompilerParams(vmem_limit_bytes=10 * 2**20),
        name="join",
    )(inside, rim, mid, coarse, from_low, from_high)


def on_device(positions, velocity, counts, tile_ids):
    held = positions.shape[0]
    capacity = positions.shape[2]
    devices = lax.axis_size("gx")
    per_peer = max(1, held // devices)
    outgoing = bucket(positions, velocity, counts, tile_ids, devices, per_peer)
    arrived = lax.all_to_all(outgoing, "gx", split_axis=0, concat_axis=0, tiled=True)
    inside, rim, mid, coarse, right, left = deposit(arrived, per_peer, capacity)
    from_low = lax.ppermute(right, "gx", [(i, (i + 1) % devices) for i in range(devices)])
    from_high = lax.ppermute(left, "gx", [(i, (i - 1) % devices) for i in range(devices)])
    return tuple(join(inside, rim, mid, coarse, from_low, from_high))


def solution(mesh):
    placed = (
        P(("snap", "gx"), None, None),
        P(("snap", "gx"), None, None),
        P(("snap", "gx")),
        P(("snap", "gx")),
    )
    return jax.shard_map(
        on_device,
        mesh=mesh,
        in_specs=placed,
        out_specs=(
            P(None, ("snap", "gx"), None, None),
            P(None, ("snap", "gx"), None),
            P(None, ("snap", "gx"), None),
        ),
        check_vma=False,
    )
```

time: 262 us -> 57 us (0.22); the launches traced: 259 us -> 56.8 us
  local copies, waits for them, and re-layouts: 146 us -> 3.29 us
  other arithmetic: 50.1 us -> 0 us
  starting transfers between devices: 21.1 us -> 0.56 us
  blocking collectives: 0 us -> 20.1 us
  Pallas kernels: 0 us -> 19.7 us
  waiting for transfers between devices: 30.3 us -> 12.5 us
  matrix products: 10.6 us -> 0 us
    slice x40 -> x0, local copies, waits for them, and re-layouts: 69.4 us -> none  [the longest x2 40.2 us: assemble(): overflow = arranged[..., TILE]]
    all_to_all x0 -> x1, blocking collectives: none -> 20.1 us  [on_device(): lax.all_to_all(outgoing, 'gx', split_axis=0, concat_axis=0, tiled=True)]
    add x7 -> x0, other arithmetic: 20 us -> none  [the longest x1 17.7 us: assemble(): interior[..., :1] + jnp.roll(overflow, 1, axis=4)[..., None]]
    pallas_call x0 -> x3, Pallas kernels: none -> 19.7 us  [the longest x1 17 us: deposit(): pl.pallas_call(functools.partial(deposit_kernel, per_peer, capacity // LA...]
    broadcast_in_dim x1 -> x0, local copies, waits for them, and re-layouts: 19.7 us -> none  [assemble(): jnp.roll(overflow, 1, axis=4)[..., None]]
    another operation x3 -> x0, local copies, waits for them, and re-layouts: 15.1 us -> none  [the longest x1 14.2 us: assemble(): tile_cells.reshape(rows_y, rows_z, 4, rim_cells, rim_cells, rim_cells)]
    concatenate x4 -> x0, other arithmetic: 14.8 us -> none  [the longest x1 13.6 us: assemble(): jnp.concatenate([interior[:, :, :, :1] + jnp.roll(overflow, 1, axis=2)[:,...]
    all_to_all x2 -> x0, waiting for transfers between devices: 13.9 us -> none  [the longest x1 13.9 us: on_device(): lax.all_to_all(outgoing, 'gx', split_axis=0, concat_axis=0, tiled=True)]
  transfers between devices with their start and end apart: 9 -> 2, of which waited for: 7 -> 1; matrix products, arithmetic and copies ran while one was open for 4% -> 0% of each run, Pallas kernels for 0% -> 0%
where the time goes in v1:
time: 57 us; the launch traced here: 56.8 us
  blocking collectives  20.1 us (35%)
  Pallas kernels  19.7 us (35%)
  waiting for transfers between devices  12.5 us (22%)
  local copies, waits for them, and re-layouts  3.29 us (6%)
  between operations  0.68 us (1%)
    all_to_all x1, blocking collectives, on_device(): lax.all_to_all(outgoing, 'gx', split_axis=0, concat_axis=0, tiled=True)  20.1 us
    pallas_call x1, Pallas kernels, deposit(): pl.pallas_call(functools.partial(deposit_kernel, per_peer, capacity // LA...  17 us
    ppermute x1, waiting for transfers between devices, on_device(): lax.ppermute(left, 'gx', [(i, (i - 1) % devices) for i in range(devices)])  12.5 us
    unnamed x12, local copies, waits for them, and re-layouts  3.29 us
    pallas_call x1, Pallas kernels, join(): pl.pallas_call(join_kernel, out_shape=[jax.ShapeDtypeStruct((4, TILE, NY,...  1.65 us
  transfers between devices with their start and end apart: 2, of which 1 were waited for; matrix products, arithmetic and copies ran while one was open for 0% of the time, Pallas kernels for 0%

profile of v1, /device:TPU:1, one launch (start us, length us, event | category | flops | bytes accessed | tf_op | source)
XLA Modules:
  0.0 56.8 jit_solution(7641308776040892228)
XLA Ops:
  0.6 0.0 copy-start.1
  0.6 0.0 copy-start
  0.7 0.0 copy-start.2
  0.7 1.0 %copy-done.2 = f32[32,3,512]{2,0,1:T(8,128)S(1)} copy-done((f32[32,3,512]{2,0,1:T(8,128)S(1)}, f32[32,3,512]{2,0,1:T(8,128)}, u32[]{:S(2)}) %copy-start.2) | copy-done | bytes 196632
  1.7 0.0 copy-start.3
  1.7 0.9 %copy-done.3 = f32[32,3,512]{2,0,1:T(8,128)S(1)} copy-done((f32[32,3,512]{2,0,1:T(8,128)S(1)}, f32[32,3,512]{2,0,1:T(8,128)}, u32[]{:S(2)}) %copy-start.3) | copy-done | bytes 196632
  2.6 0.0 copy-start.4
  2.6 0.7 %copy-done.4 = s32[32]{0:T(128)S(1)} copy-done((s32[32]{0:T(128)S(1)}, s32[32]{0:T(128)}, u32[]{:S(2)}) %copy-start.4) | copy-done | bytes 152
  3.3 0.0 copy-start.5
  3.3 0.7 %copy-done.5 = s32[32]{0:T(128)S(1)} copy-done((s32[32]{0:T(128)S(1)}, s32[32]{0:T(128)}, u32[]{:S(2)}) %copy-start.5) | copy-done | bytes 152
  3.9 1.0 %bucket.1 = f32[16,56,128]{2,1,0:T(8,128)S(1)} custom-call(s32[32]{0:T(128)S(1)} %copy-done.4, s32[32]{0:T(128)S(1)} %copy-done.5, f32[3,32,512]{2,1,0:T(8,128)S(1)} %bitcast.2, f32[3,32,512]{2,1,0:T(8,128)S(1)} %bitcast.3), custom_call_target="tpu_custom_call" | custom-call | tf_op jit(solution)/shard_map/bucket/pallas_call | solution.py:156
  5.0 20.1 %all_to_all.5.arrived_ref = f32[16,56,128]{2,1,0:T(8,128)S(1)} all-to-all(f32[16,56,128]{2,1,0:T(8,128)S(1)} %bucket.1), channel_id=1, replica_groups=mesh['snap'=2,'gx'=16] {'gx'}, dimensions={0} | all-to-all | bytes 917504 | tf_op jit(solution)/shard_map/all_to_all | solution.py:520
  25.1 0.0 copy-done.1
  25.1 0.0 copy-done
  25.1 17.0 %deposit.1 = (f32[4,16,32,256]{3,2,1,0:T(8,128)}, f32[4,5,32,256]{3,2,1,0:T(8,128)S(1)}, f32[4,128,128]{2,1,0:T(8,128)S(1)}, f32[4,32,128]{2,1,0:T(8,128)S(1)}, ...) custom-call(f32[16,56,128]{2,1,0:T(8,128)S(1)} %all_to_all.5.arrived_ref, bf16[2,512,512]{2,1,0:T(8,128)(2,1)S(1)} %copy-done, ...), custom_call_target="tpu_custom_call" | custom-call | tf_op jit(solution)/shard_map/deposit/pallas_call | solution.py:408
  42.1 0.4 collective-permute-start
  42.5 0.1 collective-permute-start.1
  42.6 12.5 %collective-permute-done.1.high_ref = f32[704,128]{1,0:T(8,128)S(1)} collective-permute-done((f32[704,128]{1,0:T(8,128)S(1)}, f32[704,128]{1,0:T(8,128)S(1)}, u32[]{:S(2)}, u32[]{:S(2)}) %collective-permute-start.1) | collective-permute-done | bytes 360480 | tf_op jit(solution)/shard_map/ppermute | solution.py:523
  55.1 0.0 collective-permute-done.low_ref
  55.1 1.6 %join.1 = (f32[4,16,32,256]{3,2,1,0:T(8,128)}, f32[4,8,2048]{2,1,0:T(8,128)}, f32[4,4,512]{2,1,0:T(4,128)}) custom-call(f32[4,16,32,256]{3,2,1,0:T(8,128)} %get-tuple-element.9.inside_ref, f32[4,5,32,256]{3,2,1,0:T(8,128)S(1)} %get-tuple-element.10.rim_ref, f32[4,128,128]{2,1,0:T(8,128)S(1)} %get-tuple-element.11.mid_in_ref, ...), custom_call_target="tpu_custom_call", output_to_operand_aliasing={{0}: (0, {})} | custom-call | tf_op jit(solution)/shard_map/join/pallas_call | solution.py:493
Async XLA Ops:
  0.6 24.4 %copy-start.1 = (bf16[280,1088]{1,0:T(8,128)(2,1)S(1)}, bf16[280,1088]{1,0:T(8,128)(2,1)}, u32[]{:S(2)}) copy-start(bf16[280,1088]{1,0:T(8,128)(2,1)} %constant.5.clone.plane_ref) | copy-start | bytes 1827844
  0.6 24.4 %copy-start = (bf16[2,512,512]{2,1,0:T(8,128)(2,1)S(1)}, bf16[2,512,512]{2,1,0:T(8,128)(2,1)}, u32[]{:S(2)}) copy-start(bf16[2,512,512]{2,1,0:T(8,128)(2,1)} %constant.4.clone.depth_ref) | copy-start | bytes 3145732
  0.7 1.1 %copy-start.2 = (f32[32,3,512]{2,0,1:T(8,128)S(1)}, f32[32,3,512]{2,0,1:T(8,128)}, u32[]{:S(2)}) copy-start(f32[32,3,512]{2,0,1:T(8,128)} %param.6) | copy-start | bytes 589828
  1.7 0.9 %copy-start.3 = (f32[32,3,512]{2,0,1:T(8,128)S(1)}, f32[32,3,512]{2,0,1:T(8,128)}, u32[]{:S(2)}) copy-start(f32[32,3,512]{2,0,1:T(8,128)} %param.7) | copy-start | bytes 589828
  2.6 0.7 %copy-start.4 = (s32[32]{0:T(128)S(1)}, s32[32]{0:T(128)}, u32[]{:S(2)}) copy-start(s32[32]{0:T(128)} %ids_ref.1) | copy-start | bytes 388
  3.3 0.7 %copy-start.5 = (s32[32]{0:T(128)S(1)}, s32[32]{0:T(128)}, u32[]{:S(2)}) copy-start(s32[32]{0:T(128)} %counts_ref.1) | copy-start | bytes 388
  42.1 13.1 %collective-permute-start = (f32[1056,128]{1,0:T(8,128)S(1)}, f32[1056,128]{1,0:T(8,128)S(1)}, u32[]{:S(2)}, u32[]{:S(2)}) collective-permute-start(f32[1056,128]{1,0:T(8,128)S(1)} %get-tuple-element.13), channel_id=1, source_target_pairs={{0,1},{1,2},{2,3},{3,4},{4,5},{5,6},{6,7},{7,8},{8,9},{9,10},{10,1... | collective-permute-start | bytes 1622024 | tf_op jit(solution)/shard_map/ppermute | solution.py:522
  42.5 12.6 %collective-permute-start.1 = (f32[704,128]{1,0:T(8,128)S(1)}, f32[704,128]{1,0:T(8,128)S(1)}, u32[]{:S(2)}, u32[]{:S(2)}) collective-permute-start(f32[704,128]{1,0:T(8,128)S(1)} %get-tuple-element.14), channel_id=1, source_target_pairs={{0,15},{1,0},{2,1},{3,2},{4,3},{5,4},{6,5},{7,6},{8,7},{9,8},{10,9... | collective-permute-start | bytes 1081352 | tf_op jit(solution)/shard_map/ppermute | solution.py:523

commit v2 on v1

--- a/solution.py
+++ b/solution.py
@@ -21,7 +21,8 @@
 QUADS = NZ // (QUAD * TILE)
 MASS_UNIT = 4.0
 DEAD = -32.0
-Y_SHIFT = 2
+BELOW = 32
+TILE_ROWS = PLANES * TILE + BELOW
 
 RIGHT = 3
 LEFT = 2
@@ -87,9 +88,8 @@
 
 
 def plane_matrix():
-    rolled = (np.arange(NY) + Y_SHIFT) % NY
-    mid_y = periodic(2, NY)[:, rolled]
-    coarse_y = periodic(3, NY)[:, rolled]
+    mid_y = periodic(2, NY)
+    coarse_y = periodic(3, NY)
     mid_x = open_ended(2, LEFT, RIGHT)
     coarse_x = open_ended(3, LEFT, RIGHT)
     rows = []
@@ -119,13 +119,31 @@
     return jnp.maximum(1.0 - jnp.abs(position - lattice), 0.0)
 
 
-def bucket_kernel(per_peer, ids_ref, counts_ref, spots_ref, speed_ref, out_ref, filled_ref):
+def bucket_kernel(
+    per_peer, ids_far, counts_far, spots_far, speed_far, out_ref,
+    filled_ref, ids_ref, counts_ref, spots_ref, speed_ref, sems,
+):
+    copies = [
+        pltpu.make_async_copy(source, target, sems.at[i])
+        for i, (source, target) in enumerate(
+            (
+                (ids_far, ids_ref),
+                (counts_far, counts_ref),
+                (spots_far, spots_ref),
+                (speed_far, speed_ref),
+            )
+        )
+    ]
+    for copy in copies:
+        copy.start()
     _, held, capacity = spots_ref.shape
     devices = out_ref.shape[0]
     chunks = capacity // LANES
     size = 6 * chunks
     for owner in range(devices):
         filled_ref[owner] = 0
+    for copy in copies:
+        copy.wait()
     if devices * per_peer > held:
         out_ref[:, per_peer * size :, :] = jnp.full((devices, 8, LANES), -1.0, jnp.float32)
 
@@ -156,15 +174,17 @@
     return pl.pallas_call(
         functools.partial(bucket_kernel, per_peer),
         out_shape=jax.ShapeDtypeStruct((devices, rows, LANES), jnp.float32),
-        in_specs=[
-            pl.BlockSpec(memory_space=pltpu.SMEM),
-            pl.BlockSpec(memory_space=pltpu.SMEM),
-            pl.BlockSpec(memory_space=pltpu.VMEM),
-            pl.BlockSpec(memory_space=pltpu.VMEM),
+        in_specs=[pl.BlockSpec(memory_space=pltpu.HBM)] * 4,
+        out_specs=pl.BlockSpec(memory_space=pltpu.VMEM),
+        scratch_shapes=[
+            pltpu.SMEM((devices,), jnp.int32),
+            pltpu.SMEM(tile_ids.shape, jnp.int32),
+            pltpu.SMEM(counts.shape, jnp.int32),
+            pltpu.VMEM((3,) + positions.shape[::2], jnp.float32),
+            pltpu.VMEM((3,) + positions.shape[::2], jnp.float32),
+            pltpu.SemaphoreType.DMA((4,)),
         ],
-        out_specs=pl.BlockSpec(memory_space=pltpu.VMEM),
-        scratch_shapes=[pltpu.SMEM((devices,), jnp.int32)],
-        compiler_params=pltpu.CompilerParams(vmem_limit_bytes=6 * 2**20),
+        compiler_params=pltpu.CompilerParams(vmem_limit_bytes=60 * 2**20),
         name="bucket",
     )(tile_ids, counts, positions.transpose(1, 0, 2), velocity.transpose(1, 0, 2))
 
@@ -184,6 +204,7 @@
     slot_ref,
     marks_ref,
     planar_ref,
+    depth_rows_ref,
     sums_ref,
     spread_ref,
     rest_ref,
@@ -213,100 +234,97 @@
     def row_of(shape, dim):
         return lax.broadcasted_iota(jnp.int32, shape, dim)
 
-    def tile_terms(q, parity, t, ty, buffer):
-        local = ty * (NZ // TILE) + q * QUAD + t
-        slot = slot_ref[local]
+    depth_rows_ref[...] = jnp.zeros(depth_rows_ref.shape, jnp.bfloat16)
+    x_lattice = row_of((BELOW, LANES), 0).astype(jnp.float32)
+    cell_lattice = row_of((TILE, LANES), 0).astype(jnp.float32)
+    first_row = row_of((TILE, LANES), 0) == 0
+
+    def tile_terms(q, t, ty, buffer):
+        slot = slot_ref[ty * (NZ // TILE) + q * QUAD + t]
         device = slot // per_peer
         base = pl.multiple_of((slot % per_peer) * size, 8)
-        y_lattice = ((row_of((NY, LANES), 0) + (Y_SHIFT + TILE * ty)) % NY).astype(jnp.float32)
-        x_lattice = row_of((24, LANES), 0).astype(jnp.float32)
-        z_lattice = row_of((TILE, LANES), 0).astype(jnp.float32)
-        depth_chunks = []
         for chunk in range(chunks):
 
             def particle(a, rows):
                 line = arrived_ref[device, pl.ds(base + (6 * chunk + a), 1), :]
                 return jnp.broadcast_to(line, (rows, LANES))
 
-            weights_x = hat(particle(0, 24), x_lattice)
-            weights_y = hat(particle(1, NY), y_lattice)
-            start = ty * capacity + chunk * LANES
+            cut = slice(t * capacity + chunk * LANES, t * capacity + (chunk + 1) * LANES)
+            weights_x = hat(particle(0, BELOW), x_lattice)
+            weights_y = hat(particle(1, TILE), cell_lattice)
             for x in range(PLANES):
-                planar = jnp.broadcast_to(weights_x[x : x + 1], (NY, LANES)) * weights_y
-                planar_ref[buffer, x * NY : (x + 1) * NY, start : start + LANES] = planar.astype(
+                planar = jnp.broadcast_to(weights_x[x : x + 1], (TILE, LANES)) * weights_y
+                planar_ref[buffer, x * TILE : (x + 1) * TILE, cut] = planar.astype(jnp.bfloat16)
+            below = weights_x * jnp.maximum(particle(1, BELOW) - (TILE - 1.0), 0.0)
+            planar_ref[buffer, PLANES * TILE :, cut] = below.astype(jnp.bfloat16)
+
+            spot_z = particle(2, TILE)
+            weights_z = hat(spot_z, cell_lattice)
+            past = jnp.where(first_row, jnp.maximum(spot_z - (TILE - 1.0), 0.0), 0.0)
+            for c in range(4):
+                charge = MASS_UNIT if c == 0 else MASS_UNIT * particle(2 + c, TILE)
+                place = c ^ (q % 2)
+                at = (place * QUAD + t) * TILE
+                depth_rows_ref[buffer, at : at + TILE, cut] = (charge * weights_z).astype(
                     jnp.bfloat16
                 )
-            weights_z = hat(particle(2, TILE), z_lattice)
-            spot_z = particle(2, TILE)
-            past = jnp.where(
-                row_of((TILE, LANES), 0) == 0, jnp.maximum(spot_z - (TILE - 1.0), 0.0), 0.0
+                if t == QUAD - 1:
+                    at = (place ^ 1) * QUAD * TILE
+                else:
+                    at = at + TILE
+                depth_rows_ref[buffer, at : at + TILE, cut] = (charge * past).astype(jnp.bfloat16)
+
+    def tile_sums(q, ty, buffer):
+        for kind, cut in enumerate(
+            (slice(0, (QUAD - 1) * capacity), slice((QUAD - 1) * capacity, QUAD * capacity))
+        ):
+            sums_ref[q, kind, ty] = lax.dot_general(
+                planar_ref[buffer, :, cut],
+                depth_rows_ref[buffer, :, cut],
+                (((1,), (1,)), ((), ())),
+                preferred_element_type=jnp.float32,
             )
-            charges = [jnp.full((TILE, LANES), MASS_UNIT, jnp.float32)] + [
-                MASS_UNIT * particle(a, TILE) for a in (3, 4, 5)
-            ]
-            zero = jnp.zeros((TILE, LANES), jnp.bfloat16)
-            pieces = []
-            for place in range(4):
-                c = place ^ parity
-                inside = (charges[c] * weights_z).astype(jnp.bfloat16)
-                other = charges[c ^ 1] if t == QUAD - 1 else charges[c]
-                outside = (other * past).astype(jnp.bfloat16)
-                for block in range(QUAD):
-                    if block == t:
-                        pieces.append(inside)
-                    elif block == (t + 1) % QUAD:
-                        pieces.append(outside)
-                    else:
-                        pieces.append(zero)
-            depth_chunks.append(jnp.concatenate(pieces, axis=0))
-        return jnp.concatenate(depth_chunks, axis=1)
-
-    def pair_of_quads(h, carry):
-        for parity in range(2):
-            q = 2 * h + parity
-            for t in range(QUAD):
-                buffer = t % 2
-                depth = jnp.concatenate(
-                    [tile_terms(q, parity, t, ty, buffer) for ty in range(NY // TILE)], axis=1
-                )
-                result = lax.dot_general(
-                    planar_ref[buffer],
-                    depth,
-                    (((1,), (1,)), ((), ())),
-                    preferred_element_type=jnp.float32,
-                )
-                if t == 0:
-                    sums_ref[q, 0] = result
-                elif t == QUAD - 1:
-                    sums_ref[q, 1] = result
-                else:
-                    sums_ref[q, 0] = sums_ref[q, 0] + result
-        return carry
-
-    lax.fori_loop(0, QUADS // 2, pair_of_quads, 0)
-
-    lane = row_of((NY, LANES), 1)
-    first_half = lane < LANES // 2
-    inner = (lane % (LANES // 2)) != 0
-
-    def window(q, plane, half):
-        rows = slice(plane * NY, (plane + 1) * NY)
+
+    steps = [(q, ty) for q in range(QUADS) for ty in range(NY // TILE)]
+    for i, (q, ty) in enumerate(steps):
+        for t in range(QUAD):
+            tile_terms(q, t, ty, i % 2)
+        if i:
+            tile_sums(*steps[i - 1], (i - 1) % 2)
+    tile_sums(*steps[-1], (len(steps) - 1) % 2)
+
+    def window(q, ty, half, rows):
         cut = slice(half * LANES, (half + 1) * LANES)
-        before = (q - 1) % QUADS
-        return sums_ref[q, 0, rows, cut] + jnp.where(
-            inner, sums_ref[q, 1, rows, cut], sums_ref[before, 1, rows, cut]
+        inner = row_of((rows.stop - rows.start, LANES), 1) % (LANES // 2) != 0
+        return sums_ref[q, 0, ty, rows, cut] + jnp.where(
+            inner, sums_ref[q, 1, ty, rows, cut], sums_ref[(q - 1) % QUADS, 1, ty, rows, cut]
         )
 
+    first_half = row_of((TILE, LANES), 1) < LANES // 2
     for half in range(2):
-        for plane in range(PLANES):
-            rows = slice(plane * NY, (plane + 1) * NY)
-            for h in range(2):
-                even, odd = window(2 * h, plane, half), window(2 * h + 1, plane, half)
-                for parity in range(2):
-                    one, two = (even, odd) if parity == 0 else (odd, even)
-                    high, low = split(jnp.where(first_half, one, two))
-                    spread_ref[2 * half + parity, rows, h * LANES : (h + 1) * LANES] = high
-                    spread_ref[2 * half + parity, rows, NZ + h * LANES : NZ + (h + 1) * LANES] = low
+        for h in range(2):
+            for ty in range(NY // TILE):
+                under = slice(PLANES * TILE, PLANES * TILE + BELOW)
+                past = [window(2 * h + i, 1 - ty, half, under) for i in range(2)]
+                for plane in range(PLANES):
+                    rows = slice(plane * TILE, (plane + 1) * TILE)
+                    even, odd = (
+                        window(2 * h + i, ty, half, rows)
+                        + jnp.where(
+                            first_row,
+                            jnp.broadcast_to(past[i][plane : plane + 1], (TILE, LANES)),
+                            0.0,
+                        )
+                        for i in range(2)
+                    )
+                    rows = slice(plane * NY + ty * TILE, plane * NY + (ty + 1) * TILE)
+                    for parity in range(2):
+                        one, two = (even, odd) if parity == 0 else (odd, even)
+                        high, low = split(jnp.where(first_half, one, two))
+                        at = h * LANES
+                        spread_ref[2 * half + parity, rows, at : at + LANES] = high
+                        at += NZ
+                        spread_ref[2 * half + parity, rows, at : at + LANES] = low
 
     def inside(c):
         return pltpu.make_async_copy(
@@ -331,10 +349,10 @@
         for plane in range(-LEFT, TILE + RIGHT):
             source = plane + 2
             if source < PLANES:
-                field = levels[source * NY : (source + 1) * NY, :NZ]
-                lag = pltpu.roll(field, 2, 0)
-                twice = field + lag
-                value = twice + pltpu.roll(twice, 2, 0) + 4.0 * (pltpu.roll(twice, 1, 0) + lag)
+                value = levels[source * NY : (source + 1) * NY, :NZ]
+                for _ in range(2):
+                    either = pltpu.roll(value, 1, 0) + pltpu.roll(value, NY - 1, 0)
+                    value = either + 2.0 * value
             else:
                 value = zero
             for k in range(4):
@@ -392,7 +410,8 @@
         ]
         return carry
 
-    lax.fori_loop(0, 4, channel, 0)
+    for c in range(4):
+        channel(c, 0)
     for c in range(4):
         inside(c).wait()
 
@@ -420,8 +439,9 @@
         scratch_shapes=[
             pltpu.SMEM((NY // TILE * (NZ // TILE),), jnp.int32),
             pltpu.SMEM((devices, 8, LANES), f32),
-            pltpu.VMEM((2, ROWS, NY // TILE * capacity), jnp.bfloat16),
-            pltpu.VMEM((QUADS, 2, ROWS, WIDTH), f32),
+            pltpu.VMEM((2, TILE_ROWS, QUAD * capacity), jnp.bfloat16),
+            pltpu.VMEM((2, WIDTH, QUAD * capacity), jnp.bfloat16),
+            pltpu.VMEM((QUADS, 2, NY // TILE, TILE_ROWS, WIDTH), f32),
             pltpu.VMEM((4, ROWS, 2 * NZ), jnp.bfloat16),
             pltpu.VMEM((2, ROWS, 2 * LANES), jnp.bfloat16),
             pltpu.VMEM((4, TILE - RIGHT - LEFT, NY, NZ), f32),

time: 57 us -> 51 us (0.89)
  local copies, waits for them, and re-layouts: 3.29 us -> 0.01 us
  Pallas kernels: 19.7 us -> 16.7 us
    pallas_call x1, Pallas kernels: 17 us -> 12.7 us  [deposit(): pl.pallas_call(functools.partial(deposit_kernel, per_peer, capacity // LA...]
    unnamed x12 -> x4, local copies, waits for them, and re-layouts: 3.29 us -> 0.01 us
    pallas_call x1, Pallas kernels: 1.03 us -> 2.43 us  [bucket(): pl.pallas_call(functools.partial(bucket_kernel, per_peer), out_shape=jax....]
where the time goes in v2:
time: 51 us; the launch traced here: 50.7 us
  blocking collectives  20.3 us (40%)
  Pallas kernels  16.7 us (33%)
  waiting for transfers between devices  12.5 us (25%)
  between operations  0.67 us (1%)
  starting transfers between devices  0.56 us (1%)
    all_to_all x1, blocking collectives, on_device(): lax.all_to_all(outgoing, 'gx', split_axis=0, concat_axis=0, tiled=True)  20.3 us
    pallas_call x1, Pallas kernels, deposit(): pl.pallas_call(functools.partial(deposit_kernel, per_peer, capacity // LA...  12.7 us
    ppermute x1, waiting for transfers between devices, on_device(): lax.ppermute(left, 'gx', [(i, (i - 1) % devices) for i in range(devices)])  12.5 us
    pallas_call x1, Pallas kernels, bucket(): pl.pallas_call(functools.partial(bucket_kernel, per_peer), out_shape=jax....  2.43 us
    pallas_call x1, Pallas kernels, join(): pl.pallas_call(join_kernel, out_shape=[jax.ShapeDtypeStruct((4, TILE, NY,...  1.62 us
  transfers between devices with their start and end apart: 2, of which 1 were waited for; matrix products, arithmetic and copies ran while one was open for 0% of the time, Pallas kernels for 0%

profile of v2, /device:TPU:1, one launch (start us, length us, event | category | flops | bytes accessed | tf_op | source)
XLA Modules:
  0.0 50.7 jit_solution(3955660156418283800)
XLA Ops:
  0.6 0.0 copy-start.1
  0.6 0.0 copy-start
  0.7 2.4 %bucket.1 = f32[16,56,128]{2,1,0:T(8,128)} custom-call(s32[32]{0:T(128)} %ids_far.1, s32[32]{0:T(128)} %counts_far.1, f32[3,32,512]{2,1,0:T(8,128)} %bitcast.2, f32[3,32,512]{2,1,0:T(8,128)} %bitcast.3), custom_call_target="tpu_custom_call" | custom-call | tf_op jit(solution)/shard_map/bucket/pallas_call | solution.py:174
  3.1 20.3 %all_to_all.5.arrived_ref = f32[16,56,128]{2,1,0:T(8,128)S(1)} all-to-all(f32[16,56,128]{2,1,0:T(8,128)} %bucket.1), channel_id=1, replica_groups=mesh['snap'=2,'gx'=16] {'gx'}, dimensions={0} | all-to-all | bytes 917504 | tf_op jit(solution)/shard_map/all_to_all | solution.py:540
  23.4 0.0 copy-done.1
  23.4 0.0 copy-done
  23.4 12.7 %deposit.1 = (f32[4,16,32,256]{3,2,1,0:T(8,128)}, f32[4,5,32,256]{3,2,1,0:T(8,128)S(1)}, f32[4,128,128]{2,1,0:T(8,128)S(1)}, f32[4,32,128]{2,1,0:T(8,128)S(1)}, ...) custom-call(f32[16,56,128]{2,1,0:T(8,128)S(1)} %all_to_all.5.arrived_ref, bf16[2,512,512]{2,1,0:T(8,128)(2,1)S(1)} %copy-done, ...), custom_call_target="tpu_custom_call" | custom-call | tf_op jit(solution)/shard_map/deposit/pallas_call | solution.py:427
  36.1 0.4 collective-permute-start
  36.5 0.1 collective-permute-start.1
  36.6 12.5 %collective-permute-done.1.high_ref = f32[704,128]{1,0:T(8,128)S(1)} collective-permute-done((f32[704,128]{1,0:T(8,128)S(1)}, f32[704,128]{1,0:T(8,128)S(1)}, u32[]{:S(2)}, u32[]{:S(2)}) %collective-permute-start.1) | collective-permute-done | bytes 360480 | tf_op jit(solution)/shard_map/ppermute | solution.py:543
  49.1 0.0 collective-permute-done.low_ref
  49.1 1.6 %join.1 = (f32[4,16,32,256]{3,2,1,0:T(8,128)}, f32[4,8,2048]{2,1,0:T(8,128)}, f32[4,4,512]{2,1,0:T(4,128)}) custom-call(f32[4,16,32,256]{3,2,1,0:T(8,128)} %get-tuple-element.9.inside_ref, f32[4,5,32,256]{3,2,1,0:T(8,128)S(1)} %get-tuple-element.10.rim_ref, f32[4,128,128]{2,1,0:T(8,128)S(1)} %get-tuple-element.11.mid_in_ref, ...), custom_call_target="tpu_custom_call", output_to_operand_aliasing={{0}: (0, {})} | custom-call | tf_op jit(solution)/shard_map/join/pallas_call | solution.py:513
Async XLA Ops:
  0.6 22.7 %copy-start.1 = (bf16[280,1088]{1,0:T(8,128)(2,1)S(1)}, bf16[280,1088]{1,0:T(8,128)(2,1)}, u32[]{:S(2)}) copy-start(bf16[280,1088]{1,0:T(8,128)(2,1)} %constant.5.clone.plane_ref) | copy-start | bytes 1827844
  0.6 22.7 %copy-start = (bf16[2,512,512]{2,1,0:T(8,128)(2,1)S(1)}, bf16[2,512,512]{2,1,0:T(8,128)(2,1)}, u32[]{:S(2)}) copy-start(bf16[2,512,512]{2,1,0:T(8,128)(2,1)} %constant.4.clone.depth_ref) | copy-start | bytes 3145732
  36.1 13.1 %collective-permute-start = (f32[1056,128]{1,0:T(8,128)S(1)}, f32[1056,128]{1,0:T(8,128)S(1)}, u32[]{:S(2)}, u32[]{:S(2)}) collective-permute-start(f32[1056,128]{1,0:T(8,128)S(1)} %get-tuple-element.13), channel_id=1, source_target_pairs={{0,1},{1,2},{2,3},{3,4},{4,5},{5,6},{6,7},{7,8},{8,9},{9,10},{10,1... | collective-permute-start | bytes 1622024 | tf_op jit(solution)/shard_map/ppermute | solution.py:542
  36.5 12.6 %collective-permute-start.1 = (f32[704,128]{1,0:T(8,128)S(1)}, f32[704,128]{1,0:T(8,128)S(1)}, u32[]{:S(2)}, u32[]{:S(2)}) collective-permute-start(f32[704,128]{1,0:T(8,128)S(1)} %get-tuple-element.14), channel_id=1, source_target_pairs={{0,15},{1,0},{2,1},{3,2},{4,3},{5,4},{6,5},{7,6},{8,7},{9,8},{10,9... | collective-permute-start | bytes 1081352 | tf_op jit(solution)/shard_map/ppermute | solution.py:543

commit v3 on v2

--- a/solution.py
+++ b/solution.py
@@ -23,6 +23,9 @@
 DEAD = -32.0
 BELOW = 32
 TILE_ROWS = PLANES * TILE + BELOW
+PLANE_ROWS = 288
+DEPTH_ROWS = 4 * NZ
+FILTER_ROWS = 18 * 1024
 
 RIGHT = 3
 LEFT = 2
@@ -83,8 +86,7 @@
         axis=1,
     )
     swapped = columns[np.arange(NZ) ^ (QUAD * TILE)]
-    both = np.stack([columns, swapped])
-    return np.concatenate([both, both], axis=1).astype(ml_dtypes.bfloat16)
+    return np.concatenate([columns, columns, swapped, swapped]).astype(ml_dtypes.bfloat16)
 
 
 def plane_matrix():
@@ -106,13 +108,44 @@
     for k in list(range(-LEFT, 0)) + list(range(TILE // 4, TILE // 4 + RIGHT)):
         for y in order:
             rows.append(np.kron(coarse_x[LEFT + k], coarse_y[y]))
+    rows += [np.zeros(ROWS)] * (PLANE_ROWS - len(rows))
     high, low = split_host(np.stack(rows))
-    return np.concatenate([high, low], axis=1)
+    width = 2 * NZ
+    ends = np.zeros((PLANE_ROWS, width), ml_dtypes.bfloat16)
+    rest = ROWS - width
+    ends[:, :rest] = high[:, width:]
+    ends[:, LANES : LANES + rest] = low[:, width:]
+    return np.concatenate([high[:, :width], low[:, :width], ends])
+
+
+def filters():
+    used = np.concatenate([depth_matrix(), plane_matrix()])
+    return np.concatenate([used, np.zeros((FILTER_ROWS - len(used), used.shape[1]), used.dtype)])
 
 
 def split(value):
     high = value.astype(jnp.bfloat16)
     return high, (value - high.astype(jnp.float32)).astype(jnp.bfloat16)
+
+
+def depth_of(c):
+    return slice(c % 2 * 2 * NZ, (c % 2 + 1) * 2 * NZ)
+
+
+def smooth_rows(value):
+    for _ in range(2):
+        either = pltpu.roll(value, 1, 0) + pltpu.roll(value, value.shape[0] - 1, 0)
+        value = either + 2.0 * value
+    return value
+
+
+def along_planes(fields, plane):
+    total = None
+    for shift, tap in zip(range(-2, 3), (1.0, 4.0, 6.0, 4.0, 1.0)):
+        if plane + shift in fields:
+            term = fields[plane + shift] if tap == 1.0 else tap * fields[plane + shift]
+            total = term if total is None else total + term
+    return total
 
 
 def hat(position, lattice):
@@ -138,14 +171,14 @@
         copy.start()
     _, held, capacity = spots_ref.shape
     devices = out_ref.shape[0]
-    chunks = capacity // LANES
-    size = 6 * chunks
+    size = 6 * capacity
     for owner in range(devices):
         filled_ref[owner] = 0
     for copy in copies:
         copy.wait()
     if devices * per_peer > held:
-        out_ref[:, per_peer * size :, :] = jnp.full((devices, 8, LANES), -1.0, jnp.float32)
+        marks = (devices, 1, per_peer * LANES)
+        out_ref[:, :, per_peer * size :] = jnp.full(marks, -1.0, jnp.float32)
 
     for tile in range(held):
         tag = ids_ref[tile]
@@ -153,27 +186,26 @@
         owner = tag // held
         rank = filled_ref[owner]
         filled_ref[owner] = rank + 1
-        base = pl.multiple_of(rank * size, 8)
-        for chunk in range(chunks):
-            cut = slice(chunk * LANES, (chunk + 1) * LANES)
-            lane = lax.broadcasted_iota(jnp.int32, (1, LANES), 1) + chunk * LANES
-            for a in range(3):
-                spots = spots_ref[a, tile : tile + 1, cut]
-                if a == 0:
-                    spots = jnp.where(lane < count, spots, DEAD)
-                out_ref[owner, pl.ds(base + 6 * chunk + a, 1), :] = spots
-                speed = speed_ref[a, tile : tile + 1, cut]
-                out_ref[owner, pl.ds(base + 6 * chunk + 3 + a, 1), :] = speed
+        base = rank * size
+        alive = lax.broadcasted_iota(jnp.int32, (1, capacity), 1) < count
+        for a in range(6):
+            source = spots_ref if a < 3 else speed_ref
+            row = source[a % 3, tile : tile + 1, :]
+            if a == 0:
+                row = jnp.where(alive, row, DEAD)
+            at = pl.multiple_of(base + a * capacity, LANES)
+            out_ref[owner, :, pl.ds(at, capacity)] = row
         mark = jnp.full((1, LANES), (tag % held).astype(jnp.float32), jnp.float32)
-        out_ref[owner, pl.ds(per_peer * size + rank, 1), :] = mark
+        at = pl.multiple_of(per_peer * size + rank * LANES, LANES)
+        out_ref[owner, :, pl.ds(at, LANES)] = mark
 
 
 def bucket(positions, velocity, counts, tile_ids, devices, per_peer):
     capacity = positions.shape[2]
-    rows = per_peer * 6 * (capacity // LANES) + 8
+    columns = per_peer * (6 * capacity + LANES)
     return pl.pallas_call(
         functools.partial(bucket_kernel, per_peer),
-        out_shape=jax.ShapeDtypeStruct((devices, rows, LANES), jnp.float32),
+        out_shape=jax.ShapeDtypeStruct((devices, 1, columns), jnp.float32),
         in_specs=[pl.BlockSpec(memory_space=pltpu.HBM)] * 4,
         out_specs=pl.BlockSpec(memory_space=pltpu.VMEM),
         scratch_shapes=[
@@ -193,35 +225,39 @@
     per_peer,
     chunks,
     arrived_ref,
-    depth_ref,
-    plane_ref,
-    fine_ref,
-    rim_ref,
+    filter_far,
+    spread_ref,
     mid_ref,
     coarse_ref,
     right_ref,
     left_ref,
     slot_ref,
     marks_ref,
-    planar_ref,
-    depth_rows_ref,
+    planar_even,
+    planar_odd,
+    depth_even,
+    depth_odd,
     sums_ref,
-    spread_ref,
     rest_ref,
-    inside_ref,
+    filter_ref,
     sems,
 ):
     devices = arrived_ref.shape[0]
-    size = 6 * chunks
     capacity = chunks * LANES
-    marks = pltpu.make_async_copy(
-        arrived_ref.at[:, per_peer * size : per_peer * size + 8], marks_ref, sems.at[4]
+    size = 6 * capacity
+    marks = pltpu.make_async_copy(arrived_ref.at[:, :, per_peer * size :], marks_ref, sems.at[0])
+    marks.start()
+    fetch = pltpu.make_async_copy(
+        filter_far.at[: DEPTH_ROWS + 3 * PLANE_ROWS], filter_ref, sems.at[1]
     )
-    marks.start()
+    fetch.start()
+    planars, depths = (planar_even, planar_odd), (depth_even, depth_odd)
+    for ref in depths:
+        ref[...] = jnp.zeros(ref.shape, jnp.bfloat16)
     marks.wait()
 
     def look(slot, carry):
-        tag = marks_ref[slot // per_peer, slot % per_peer, 0].astype(jnp.int32)
+        tag = marks_ref[slot // per_peer, 0, slot % per_peer * LANES].astype(jnp.int32)
 
         @pl.when(tag >= 0)
         def _():
@@ -234,7 +270,6 @@
     def row_of(shape, dim):
         return lax.broadcasted_iota(jnp.int32, shape, dim)
 
-    depth_rows_ref[...] = jnp.zeros(depth_rows_ref.shape, jnp.bfloat16)
     x_lattice = row_of((BELOW, LANES), 0).astype(jnp.float32)
     cell_lattice = row_of((TILE, LANES), 0).astype(jnp.float32)
     first_row = row_of((TILE, LANES), 0) == 0
@@ -242,11 +277,12 @@
     def tile_terms(q, t, ty, buffer):
         slot = slot_ref[ty * (NZ // TILE) + q * QUAD + t]
         device = slot // per_peer
-        base = pl.multiple_of((slot % per_peer) * size, 8)
+        base = (slot % per_peer) * size
         for chunk in range(chunks):
 
             def particle(a, rows):
-                line = arrived_ref[device, pl.ds(base + (6 * chunk + a), 1), :]
+                at = pl.multiple_of(base + (a * capacity + chunk * LANES), LANES)
+                line = arrived_ref[device, :, pl.ds(at, LANES)]
                 return jnp.broadcast_to(line, (rows, LANES))
 
             cut = slice(t * capacity + chunk * LANES, t * capacity + (chunk + 1) * LANES)
@@ -254,9 +290,9 @@
             weights_y = hat(particle(1, TILE), cell_lattice)
             for x in range(PLANES):
                 planar = jnp.broadcast_to(weights_x[x : x + 1], (TILE, LANES)) * weights_y
-                planar_ref[buffer, x * TILE : (x + 1) * TILE, cut] = planar.astype(jnp.bfloat16)
+                planars[buffer][x * TILE : (x + 1) * TILE, cut] = planar.astype(jnp.bfloat16)
             below = weights_x * jnp.maximum(particle(1, BELOW) - (TILE - 1.0), 0.0)
-            planar_ref[buffer, PLANES * TILE :, cut] = below.astype(jnp.bfloat16)
+            planars[buffer][PLANES * TILE :, cut] = below.astype(jnp.bfloat16)
 
             spot_z = particle(2, TILE)
             weights_z = hat(spot_z, cell_lattice)
@@ -265,32 +301,32 @@
                 charge = MASS_UNIT if c == 0 else MASS_UNIT * particle(2 + c, TILE)
                 place = c ^ (q % 2)
                 at = (place * QUAD + t) * TILE
-                depth_rows_ref[buffer, at : at + TILE, cut] = (charge * weights_z).astype(
+                depths[buffer][at : at + TILE, cut] = (charge * weights_z).astype(
                     jnp.bfloat16
                 )
                 if t == QUAD - 1:
                     at = (place ^ 1) * QUAD * TILE
                 else:
                     at = at + TILE
-                depth_rows_ref[buffer, at : at + TILE, cut] = (charge * past).astype(jnp.bfloat16)
+                depths[buffer][at : at + TILE, cut] = (charge * past).astype(jnp.bfloat16)
 
     def tile_sums(q, ty, buffer):
         for kind, cut in enumerate(
             (slice(0, (QUAD - 1) * capacity), slice((QUAD - 1) * capacity, QUAD * capacity))
         ):
             sums_ref[q, kind, ty] = lax.dot_general(
-                planar_ref[buffer, :, cut],
-                depth_rows_ref[buffer, :, cut],
+                planars[buffer][:, cut],
+                depths[buffer][:, cut],
                 (((1,), (1,)), ((), ())),
                 preferred_element_type=jnp.float32,
             )
 
     steps = [(q, ty) for q in range(QUADS) for ty in range(NY // TILE)]
     for i, (q, ty) in enumerate(steps):
+        if i:
+            tile_sums(*steps[i - 1], (i - 1) % 2)
         for t in range(QUAD):
             tile_terms(q, t, ty, i % 2)
-        if i:
-            tile_sums(*steps[i - 1], (i - 1) % 2)
     tile_sums(*steps[-1], (len(steps) - 1) % 2)
 
     def window(q, ty, half, rows):
@@ -326,61 +362,53 @@
                         at += NZ
                         spread_ref[2 * half + parity, rows, at : at + LANES] = low
 
-    def inside(c):
-        return pltpu.make_async_copy(
-            inside_ref.at[c], fine_ref.at[c, RIGHT : TILE - LEFT], sems.at[c]
-        )
-
-    def channel(c, carry):
-        levels = jnp.dot(
-            spread_ref[c], depth_ref[c % 2], preferred_element_type=jnp.float32
-        )
-        coarse = levels[:, 3 * LANES :]
+    fetch.wait()
+    edge_planes = list(range(LEFT)) + list(range(PLANES - RIGHT, PLANES))
+
+    def channel(c):
+        rest = jnp.dot(spread_ref[c], filter_ref[depth_of(c), NZ:], preferred_element_type=jnp.float32)
+        coarse = rest[:, LANES:]
         coarse = coarse + pltpu.roll(coarse, LANES // 2, 1)
-        mid_high, mid_low = split(levels[:, 2 * LANES : 3 * LANES])
+        mid_high, mid_low = split(rest[:, :LANES])
         coarse_high, coarse_low = split(coarse)
         rest_ref[0, :, :LANES] = mid_high
         rest_ref[0, :, LANES:] = coarse_high
         rest_ref[1, :, :LANES] = mid_low
         rest_ref[1, :, LANES:] = coarse_low
 
-        zero = jnp.zeros((NY, NZ), jnp.float32)
-        held = [zero] * 4
-        for plane in range(-LEFT, TILE + RIGHT):
-            source = plane + 2
-            if source < PLANES:
-                value = levels[source * NY : (source + 1) * NY, :NZ]
-                for _ in range(2):
-                    either = pltpu.roll(value, 1, 0) + pltpu.roll(value, NY - 1, 0)
-                    value = either + 2.0 * value
-            else:
-                value = zero
-            for k in range(4):
-                following = value + held[k]
-                held[k] = value
-                value = following
-            if plane < 0:
-                row = (c * LEFT + plane + LEFT) * 2 * NY
-                left_ref[pl.ds(pl.multiple_of(row, 8), NY), :] = value[:, :LANES]
-                left_ref[pl.ds(pl.multiple_of(row + NY, 8), NY), :] = value[:, LANES:]
-            elif plane >= TILE:
-                row = (c * RIGHT + plane - TILE) * 2 * NY
-                right_ref[pl.ds(pl.multiple_of(row, 8), NY), :] = value[:, :LANES]
-                right_ref[pl.ds(pl.multiple_of(row + NY, 8), NY), :] = value[:, LANES:]
-            elif plane < RIGHT:
-                rim_ref[c, plane] = value
-            elif plane >= TILE - LEFT:
-                rim_ref[c, RIGHT + plane - (TILE - LEFT)] = value
-            else:
-                inside_ref[c, plane - RIGHT] = value
-
-        inside(c).start()
-        high_rows, low_rows = plane_ref[:, :ROWS], plane_ref[:, ROWS:]
-        packed = (
-            jnp.dot(high_rows, rest_ref[0], preferred_element_type=jnp.float32)
-            + jnp.dot(high_rows, rest_ref[1], preferred_element_type=jnp.float32)
-            + jnp.dot(low_rows, rest_ref[0], preferred_element_type=jnp.float32)
+        edges = jnp.dot(
+            jnp.concatenate(
+                [spread_ref[c, : LEFT * NY], spread_ref[c, (PLANES - RIGHT) * NY :]], axis=0
+            ),
+            filter_ref[depth_of(c), :NZ],
+            preferred_element_type=jnp.float32,
         )
+        fields = {
+            plane: smooth_rows(edges[i * NY : (i + 1) * NY]) for i, plane in enumerate(edge_planes)
+        }
+        for ref, planes, first in ((left_ref, LEFT, -LEFT), (right_ref, RIGHT, TILE)):
+            for i in range(planes):
+                value = along_planes(fields, first + i)
+                row = (c * planes + i) * 2 * NY
+                ref[row : row + NY, :] = value[:, :LANES]
+                ref[row + NY : row + 2 * NY, :] = value[:, LANES:]
+
+        width = 2 * NZ
+        tall = ROWS - width
+        at = DEPTH_ROWS
+        packed = None
+        for part, source in ((0, 0), (0, 1), (1, 0)):
+            rows = slice(at + part * PLANE_ROWS, at + (part + 1) * PLANE_ROWS)
+            term = jnp.dot(
+                filter_ref[rows, :], rest_ref[source, :width], preferred_element_type=jnp.float32
+            )
+            packed = term if packed is None else packed + term
+            rows = slice(at + 2 * PLANE_ROWS, at + 3 * PLANE_ROWS)
+            packed = packed + jnp.dot(
+                filter_ref[rows, part * LANES : part * LANES + tall],
+                rest_ref[source, width:],
+                preferred_element_type=jnp.float32,
+            )
         mid_rows = NY // 2 * (TILE // 2)
         mid_edge = NY // 2
         mid_ref[c] = packed[:mid_rows, :LANES]
@@ -408,48 +436,103 @@
         right_ref[pl.ds(pl.multiple_of(row, 8), RIGHT * coarse_edge), :] = packed[
             at : at + RIGHT * coarse_edge, LANES:
         ]
-        return carry
 
     for c in range(4):
-        channel(c, 0)
+        channel(c)
+
+
+def fine_kernel(spread_ref, filter_far, fine_ref, rim_ref, inside_ref, filter_ref, sems):
+    fetch = pltpu.make_async_copy(filter_far.at[:DEPTH_ROWS], filter_ref, sems.at[4])
+    fetch.start()
+    fetch.wait()
+
+    def inside(c):
+        return pltpu.make_async_copy(
+            inside_ref.at[c], fine_ref.at[c, RIGHT : TILE - LEFT], sems.at[c]
+        )
+
+    for c in range(4):
+        level = jnp.dot(spread_ref[c], filter_ref[depth_of(c), :NZ], preferred_element_type=jnp.float32)
+        zero = jnp.zeros((NY, NZ), jnp.float32)
+        held = [zero] * 4
+        for plane in range(-LEFT, TILE):
+            source = plane + 2
+            value = zero
+            if source < PLANES:
+                value = smooth_rows(level[source * NY : (source + 1) * NY])
+            for k in range(4):
+                following = value + held[k]
+                held[k] = value
+                value = following
+            if 0 <= plane < RIGHT:
+                rim_ref[c, plane] = value
+            elif plane >= TILE - LEFT:
+                rim_ref[c, RIGHT + plane - (TILE - LEFT)] = value
+            elif plane >= 0:
+                inside_ref[c, plane - RIGHT] = value
+        inside(c).start()
     for c in range(4):
         inside(c).wait()
 
 
+def fine(spread, matrices):
+    f32 = jnp.float32
+    vmem = pl.BlockSpec(memory_space=pltpu.VMEM)
+    return pl.pallas_call(
+        fine_kernel,
+        out_shape=[
+            jax.ShapeDtypeStruct((4, TILE, NY, NZ), f32),
+            jax.ShapeDtypeStruct((4, RIGHT + LEFT, NY, NZ), f32),
+        ],
+        in_specs=[vmem, pl.BlockSpec(memory_space=pltpu.HBM)],
+        out_specs=[pl.BlockSpec(memory_space=pl.ANY), vmem],
+        scratch_shapes=[
+            pltpu.VMEM((4, TILE - RIGHT - LEFT, NY, NZ), f32),
+            pltpu.VMEM((DEPTH_ROWS, 2 * NZ), jnp.bfloat16),
+            pltpu.SemaphoreType.DMA((5,)),
+        ],
+        compiler_params=pltpu.CompilerParams(vmem_limit_bytes=44 * 2**20),
+        cost_estimate=pl.CostEstimate(
+            flops=4 * 2 * ROWS * 2 * NZ * NZ, bytes_accessed=10**7, transcendentals=0
+        ),
+        name="fine",
+    )(spread, matrices)
+
+
 def edge_rows(planes):
     return 4 * planes * (2 * NY + NY // 2 + NY // 4)
 
 
-def deposit(arrived, per_peer, capacity):
+def deposit(arrived, matrices, per_peer, capacity):
     devices = arrived.shape[0]
     f32 = jnp.float32
     vmem = pl.BlockSpec(memory_space=pltpu.VMEM)
     return pl.pallas_call(
         functools.partial(deposit_kernel, per_peer, capacity // LANES),
         out_shape=[
-            jax.ShapeDtypeStruct((4, TILE, NY, NZ), f32),
-            jax.ShapeDtypeStruct((4, RIGHT + LEFT, NY, NZ), f32),
+            jax.ShapeDtypeStruct((4, ROWS, 2 * NZ), jnp.bfloat16),
             jax.ShapeDtypeStruct((4, NY // 2 * (TILE // 2), LANES), f32),
             jax.ShapeDtypeStruct((4, NY // 4 * (TILE // 4), LANES), f32),
             jax.ShapeDtypeStruct((edge_rows(RIGHT), LANES), f32),
             jax.ShapeDtypeStruct((edge_rows(LEFT), LANES), f32),
         ],
-        in_specs=[vmem] * 3,
-        out_specs=[pl.BlockSpec(memory_space=pl.ANY)] + [vmem] * 5,
+        in_specs=[vmem, pl.BlockSpec(memory_space=pltpu.HBM)],
+        out_specs=[vmem] * 5,
         scratch_shapes=[
             pltpu.SMEM((NY // TILE * (NZ // TILE),), jnp.int32),
-            pltpu.SMEM((devices, 8, LANES), f32),
-            pltpu.VMEM((2, TILE_ROWS, QUAD * capacity), jnp.bfloat16),
-            pltpu.VMEM((2, WIDTH, QUAD * capacity), jnp.bfloat16),
+            pltpu.SMEM((devices, 1, per_peer * LANES), f32),
+            pltpu.VMEM((TILE_ROWS, QUAD * capacity), jnp.bfloat16),
+            pltpu.VMEM((TILE_ROWS, QUAD * capacity), jnp.bfloat16),
+            pltpu.VMEM((WIDTH, QUAD * capacity), jnp.bfloat16),
+            pltpu.VMEM((WIDTH, QUAD * capacity), jnp.bfloat16),
             pltpu.VMEM((QUADS, 2, NY // TILE, TILE_ROWS, WIDTH), f32),
-            pltpu.VMEM((4, ROWS, 2 * NZ), jnp.bfloat16),
             pltpu.VMEM((2, ROWS, 2 * LANES), jnp.bfloat16),
-            pltpu.VMEM((4, TILE - RIGHT - LEFT, NY, NZ), f32),
-            pltpu.SemaphoreType.DMA((5,)),
-        ],
-        compiler_params=pltpu.CompilerParams(vmem_limit_bytes=28 * 2**20),
+            pltpu.VMEM((DEPTH_ROWS + 3 * PLANE_ROWS, 2 * NZ), jnp.bfloat16),
+            pltpu.SemaphoreType.DMA((2,)),
+        ],
+        compiler_params=pltpu.CompilerParams(vmem_limit_bytes=44 * 2**20),
         name="deposit",
-    )(arrived, jnp.asarray(depth_matrix()), jnp.asarray(plane_matrix()))
+    )(arrived, matrices)
 
 
 def join_kernel(
@@ -536,11 +619,13 @@
     capacity = positions.shape[2]
     devices = lax.axis_size("gx")
     per_peer = max(1, held // devices)
+    matrices = jnp.asarray(filters())
     outgoing = bucket(positions, velocity, counts, tile_ids, devices, per_peer)
     arrived = lax.all_to_all(outgoing, "gx", split_axis=0, concat_axis=0, tiled=True)
-    inside, rim, mid, coarse, right, left = deposit(arrived, per_peer, capacity)
+    spread, mid, coarse, right, left = deposit(arrived, matrices, per_peer, capacity)
     from_low = lax.ppermute(right, "gx", [(i, (i + 1) % devices) for i in range(devices)])
     from_high = lax.ppermute(left, "gx", [(i, (i - 1) % devices) for i in range(devices)])
+    inside, rim = fine(spread, matrices)
     return tuple(join(inside, rim, mid, coarse, from_low, from_high))
 
 

time: 51 us -> 48.2 us (0.945)
  waiting for transfers between devices: 12.5 us -> 8.36 us
  Pallas kernels: 16.7 us -> 18.8 us
  blocking collectives: 20.3 us -> 19.5 us
    ppermute x1, waiting for transfers between devices: 12.5 us -> 8.35 us  [on_device(): lax.ppermute(left, 'gx', [(i, (i - 1) % devices) for i in range(devices)])]
    pallas_call x0 -> x1, Pallas kernels: none -> 4.01 us  [fine(): pl.pallas_call(fine_kernel, out_shape=[jax.ShapeDtypeStruct((4, TILE, NY,...]
    pallas_call x1, Pallas kernels: 12.7 us -> 10.9 us  [deposit(): pl.pallas_call(functools.partial(deposit_kernel, per_peer, capacity // LA...]
    all_to_all x1, blocking collectives: 20.3 us -> 19.5 us  [on_device(): lax.all_to_all(outgoing, 'gx', split_axis=0, concat_axis=0, tiled=True)]
  transfers between devices with their start and end apart: 2 -> 2, of which waited for: 1 -> 1; matrix products, arithmetic and copies ran while one was open for 0% -> 0% of each run, Pallas kernels for 0% -> 8%
where the time goes in v3:
time: 48.2 us; the launch traced here: 47.9 us
  blocking collectives  19.5 us (40%)
  Pallas kernels  18.8 us (39%)
  waiting for transfers between devices  8.36 us (17%)
  between operations  0.66 us (1%)
  starting transfers between devices  0.56 us (1%)
    all_to_all x1, blocking collectives, on_device(): lax.all_to_all(outgoing, 'gx', split_axis=0, concat_axis=0, tiled=True)  19.5 us
    pallas_call x1, Pallas kernels, deposit(): pl.pallas_call(functools.partial(deposit_kernel, per_peer, capacity // LA...  10.9 us
    ppermute x1, waiting for transfers between devices, on_device(): lax.ppermute(left, 'gx', [(i, (i - 1) % devices) for i in range(devices)])  8.35 us
    pallas_call x1, Pallas kernels, fine(): pl.pallas_call(fine_kernel, out_shape=[jax.ShapeDtypeStruct((4, TILE, NY,...  4.01 us
    pallas_call x1, Pallas kernels, bucket(): pl.pallas_call(functools.partial(bucket_kernel, per_peer), out_shape=jax....  2.3 us
    pallas_call x1, Pallas kernels, join(): pl.pallas_call(join_kernel, out_shape=[jax.ShapeDtypeStruct((4, TILE, NY,...  1.62 us
  transfers between devices with their start and end apart: 2, of which 1 were waited for; matrix products, arithmetic and copies ran while one was open for 0% of the time, Pallas kernels for 8%

profile of v3, /device:TPU:1, one launch (start us, length us, event | category | flops | bytes accessed | tf_op | source)
XLA Modules:
  0.0 47.9 jit_solution(17471634407893993210)
XLA Ops:
  0.6 2.3 %bucket.1 = f32[16,1,6400]{2,1,0:T(1,128)} custom-call(s32[32]{0:T(128)} %ids_far.1, s32[32]{0:T(128)} %counts_far.1, f32[3,32,512]{2,1,0:T(8,128)} %bitcast.2, f32[3,32,512]{2,1,0:T(8,128)} %bitcast.3), custom_call_target="tpu_custom_call" | custom-call | tf_op jit(solution)/shard_map/bucket/pallas_call | solution.py:206
  2.9 19.5 %all_to_all.5.arrived_ref = f32[16,1,6400]{2,1,0:T(1,128)S(1)} all-to-all(f32[16,1,6400]{2,1,0:T(1,128)} %bucket.1), channel_id=1, replica_groups=mesh['snap'=2,'gx'=16] {'gx'}, dimensions={0} | all-to-all | bytes 819200 | tf_op jit(solution)/shard_map/all_to_all | solution.py:624
  22.4 10.9 %deposit.1 = (bf16[4,544,512]{2,1,0:T(8,128)(2,1)S(1)}, f32[4,128,128]{2,1,0:T(8,128)S(1)}, f32[4,32,128]{2,1,0:T(8,128)S(1)}, f32[1056,128]{1,0:T(8,128)S(1)}, f32[704,128]{1,0:T(8,128)S(1)}) custom-call(f32[16,1,6400]{2,1,0:T(1,128)S(1)} %all_to_all.5.arrived_ref, bf16[18432,512]{1,0:T(8,128)(2,1)} %constant.2.clone.filter_far), custom_call_target="tpu_custom_call" | custom-call | tf_op jit(solution)/shard_map/deposit/pallas_call | solution.py:510
  33.4 0.3 collective-permute-start
  33.6 0.3 collective-permute-start.1
  33.9 4.0 %fine.1 = (f32[4,16,32,256]{3,2,1,0:T(8,128)}, f32[4,5,32,256]{3,2,1,0:T(8,128)S(1)}) custom-call(bf16[4,544,512]{2,1,0:T(8,128)(2,1)S(1)} %get-tuple-element.10.spread_ref, bf16[18432,512]{1,0:T(8,128)(2,1)} %constant.2.clone.filter_far), custom_call_target="tpu_custom_call" | custom-call | flops 570425344 | bytes 10000000 | tf_op jit(solution)/shard_map/fine/pallas_call | solution.py:481
  37.9 8.4 %collective-permute-done.1.high_ref = f32[704,128]{1,0:T(8,128)S(1)} collective-permute-done((f32[704,128]{1,0:T(8,128)S(1)}, f32[704,128]{1,0:T(8,128)S(1)}, u32[]{:S(2)}, u32[]{:S(2)}) %collective-permute-start.1) | collective-permute-done | bytes 360480 | tf_op jit(solution)/shard_map/ppermute | solution.py:627
  46.3 0.0 collective-permute-done.low_ref
  46.3 1.6 %join.1 = (f32[4,16,32,256]{3,2,1,0:T(8,128)}, f32[4,8,2048]{2,1,0:T(8,128)}, f32[4,4,512]{2,1,0:T(4,128)}) custom-call(f32[4,16,32,256]{3,2,1,0:T(8,128)} %get-tuple-element.11.inside_ref, f32[4,5,32,256]{3,2,1,0:T(8,128)S(1)} %get-tuple-element.12.rim_ref, f32[4,128,128]{2,1,0:T(8,128)S(1)} %get-tuple-element.13.mid_in_ref, ...), custom_call_target="tpu_custom_call", output_to_operand_aliasing={{0}: (0, {})} | custom-call | tf_op jit(solution)/shard_map/join/pallas_call | solution.py:596
Async XLA Ops:
  33.4 12.9 %collective-permute-start = (f32[1056,128]{1,0:T(8,128)S(1)}, f32[1056,128]{1,0:T(8,128)S(1)}, u32[]{:S(2)}, u32[]{:S(2)}) collective-permute-start(f32[1056,128]{1,0:T(8,128)S(1)} %get-tuple-element.15), channel_id=1, source_target_pairs={{0,1},{1,2},{2,3},{3,4},{4,5},{5,6},{6,7},{7,8},{8,9},{9,10},{10,1... | collective-permute-start | bytes 1622024 | tf_op jit(solution)/shard_map/ppermute | solution.py:626
  33.6 12.6 %collective-permute-start.1 = (f32[704,128]{1,0:T(8,128)S(1)}, f32[704,128]{1,0:T(8,128)S(1)}, u32[]{:S(2)}, u32[]{:S(2)}) collective-permute-start(f32[704,128]{1,0:T(8,128)S(1)} %get-tuple-element.16), channel_id=1, source_target_pairs={{0,15},{1,0},{2,1},{3,2},{4,3},{5,4},{6,5},{7,6},{8,7},{9,8},{10,9... | collective-permute-start | bytes 1081352 | tf_op jit(solution)/shard_map/ppermute | solution.py:627

commit v4 on v3

--- a/solution.py
+++ b/solution.py
@@ -113,8 +113,8 @@
     width = 2 * NZ
     ends = np.zeros((PLANE_ROWS, width), ml_dtypes.bfloat16)
     rest = ROWS - width
-    ends[:, :rest] = high[:, width:]
-    ends[:, LANES : LANES + rest] = low[:, width:]
+    for i, part in enumerate((high, high, low)):
+        ends[:, i * rest : (i + 1) * rest] = part[:, width:]
     return np.concatenate([high[:, :width], low[:, :width], ends])
 
 
@@ -239,6 +239,7 @@
     depth_odd,
     sums_ref,
     rest_ref,
+    tails_ref,
     filter_ref,
     sems,
 ):
@@ -256,16 +257,18 @@
         ref[...] = jnp.zeros(ref.shape, jnp.bfloat16)
     marks.wait()
 
+    tiles = NY // TILE * (NZ // TILE)
+
     def look(slot, carry):
         tag = marks_ref[slot // per_peer, 0, slot % per_peer * LANES].astype(jnp.int32)
-
-        @pl.when(tag >= 0)
-        def _():
-            slot_ref[tag] = slot
-
+        slot_ref[jnp.where(tag < 0, tiles, tag)] = slot
         return carry
 
-    lax.fori_loop(0, devices * per_peer, look, 0)
+    if devices * per_peer == tiles:
+        for slot in range(tiles):
+            look(slot, 0)
+    else:
+        lax.fori_loop(0, devices * per_peer, look, 0)
 
     def row_of(shape, dim):
         return lax.broadcasted_iota(jnp.int32, shape, dim)
@@ -365,16 +368,24 @@
     fetch.wait()
     edge_planes = list(range(LEFT)) + list(range(PLANES - RIGHT, PLANES))
 
+    width = 2 * NZ
+    tall = ROWS - width
+
     def channel(c):
         rest = jnp.dot(spread_ref[c], filter_ref[depth_of(c), NZ:], preferred_element_type=jnp.float32)
         coarse = rest[:, LANES:]
         coarse = coarse + pltpu.roll(coarse, LANES // 2, 1)
         mid_high, mid_low = split(rest[:, :LANES])
         coarse_high, coarse_low = split(coarse)
-        rest_ref[0, :, :LANES] = mid_high
-        rest_ref[0, :, LANES:] = coarse_high
-        rest_ref[1, :, :LANES] = mid_low
-        rest_ref[1, :, LANES:] = coarse_low
+        for i, (mid, rough) in enumerate(((mid_high, coarse_high), (mid_low, coarse_low))):
+            rest_ref[c, i, :, :LANES] = mid[:width]
+            rest_ref[c, i, :, LANES:] = rough[:width]
+        for i, (mid, rough) in enumerate(
+            ((mid_high, coarse_high), (mid_low, coarse_low), (mid_high, coarse_high))
+        ):
+            rows = slice(i * tall, (i + 1) * tall)
+            tails_ref[c, rows, :LANES] = mid[width:]
+            tails_ref[c, rows, LANES:] = rough[width:]
 
         edges = jnp.dot(
             jnp.concatenate(
@@ -393,20 +404,18 @@
                 ref[row : row + NY, :] = value[:, :LANES]
                 ref[row + NY : row + 2 * NY, :] = value[:, LANES:]
 
-        width = 2 * NZ
-        tall = ROWS - width
-        at = DEPTH_ROWS
-        packed = None
+    def planes(c):
+        at = DEPTH_ROWS + 2 * PLANE_ROWS
+        packed = jnp.dot(
+            filter_ref[at : at + PLANE_ROWS, : 3 * tall],
+            tails_ref[c],
+            preferred_element_type=jnp.float32,
+        )
         for part, source in ((0, 0), (0, 1), (1, 0)):
-            rows = slice(at + part * PLANE_ROWS, at + (part + 1) * PLANE_ROWS)
-            term = jnp.dot(
-                filter_ref[rows, :], rest_ref[source, :width], preferred_element_type=jnp.float32
-            )
-            packed = term if packed is None else packed + term
-            rows = slice(at + 2 * PLANE_ROWS, at + 3 * PLANE_ROWS)
+            at = DEPTH_ROWS + part * PLANE_ROWS
             packed = packed + jnp.dot(
-                filter_ref[rows, part * LANES : part * LANES + tall],
-                rest_ref[source, width:],
+                filter_ref[at : at + PLANE_ROWS, :],
+                rest_ref[c, source],
                 preferred_element_type=jnp.float32,
             )
         mid_rows = NY // 2 * (TILE // 2)
@@ -437,8 +446,11 @@
             at : at + RIGHT * coarse_edge, LANES:
         ]
 
+    channel(0)
     for c in range(4):
-        channel(c)
+        if c < 3:
+            channel(c + 1)
+        planes(c)
 
 
 def fine_kernel(spread_ref, filter_far, fine_ref, rim_ref, inside_ref, filter_ref, sems):
@@ -519,14 +531,15 @@
         in_specs=[vmem, pl.BlockSpec(memory_space=pltpu.HBM)],
         out_specs=[vmem] * 5,
         scratch_shapes=[
-            pltpu.SMEM((NY // TILE * (NZ // TILE),), jnp.int32),
+            pltpu.SMEM((NY // TILE * (NZ // TILE) + 1,), jnp.int32),
             pltpu.SMEM((devices, 1, per_peer * LANES), f32),
             pltpu.VMEM((TILE_ROWS, QUAD * capacity), jnp.bfloat16),
             pltpu.VMEM((TILE_ROWS, QUAD * capacity), jnp.bfloat16),
             pltpu.VMEM((WIDTH, QUAD * capacity), jnp.bfloat16),
             pltpu.VMEM((WIDTH, QUAD * capacity), jnp.bfloat16),
             pltpu.VMEM((QUADS, 2, NY // TILE, TILE_ROWS, WIDTH), f32),
-            pltpu.VMEM((2, ROWS, 2 * LANES), jnp.bfloat16),
+            pltpu.VMEM((4, 2, 2 * NZ, 2 * LANES), jnp.bfloat16),
+            pltpu.VMEM((4, 3 * (ROWS - 2 * NZ), 2 * LANES), jnp.bfloat16),
             pltpu.VMEM((DEPTH_ROWS + 3 * PLANE_ROWS, 2 * NZ), jnp.bfloat16),
             pltpu.SemaphoreType.DMA((2,)),
         ],

time: 48.2 us -> 46.8 us (0.971)
  Pallas kernels: 18.8 us -> 17.5 us
    pallas_call x1, Pallas kernels: 10.9 us -> 9.54 us  [deposit(): pl.pallas_call(functools.partial(deposit_kernel, per_peer, capacity // LA...]
  transfers between devices with their start and end apart: 2 -> 2, of which waited for: 1 -> 1; matrix products, arithmetic and copies ran while one was open for 0% -> 0% of each run, Pallas kernels for 8% -> 9%
where the time goes in v4:
time: 46.8 us; the launch traced here: 46.5 us
  blocking collectives  19.5 us (42%)
  Pallas kernels  17.5 us (37%)
  waiting for transfers between devices  8.35 us (18%)
  between operations  0.66 us (1%)
  starting transfers between devices  0.56 us (1%)
    all_to_all x1, blocking collectives, on_device(): lax.all_to_all(outgoing, 'gx', split_axis=0, concat_axis=0, tiled=True)  19.5 us
    pallas_call x1, Pallas kernels, deposit(): pl.pallas_call(functools.partial(deposit_kernel, per_peer, capacity // LA...  9.54 us
    ppermute x1, waiting for transfers between devices, on_device(): lax.ppermute(left, 'gx', [(i, (i - 1) % devices) for i in range(devices)])  8.35 us
    pallas_call x1, Pallas kernels, fine(): pl.pallas_call(fine_kernel, out_shape=[jax.ShapeDtypeStruct((4, TILE, NY,...  4.01 us
    pallas_call x1, Pallas kernels, bucket(): pl.pallas_call(functools.partial(bucket_kernel, per_peer), out_shape=jax....  2.3 us
    pallas_call x1, Pallas kernels, join(): pl.pallas_call(join_kernel, out_shape=[jax.ShapeDtypeStruct((4, TILE, NY,...  1.62 us
  transfers between devices with their start and end apart: 2, of which 1 were waited for; matrix products, arithmetic and copies ran while one was open for 0% of the time, Pallas kernels for 9%

profile of v4, /device:TPU:1, one launch (start us, length us, event | category | flops | bytes accessed | tf_op | source)
XLA Modules:
  0.0 46.5 jit_solution(15297908349520869003)
XLA Ops:
  0.6 2.3 %bucket.1 = f32[16,1,6400]{2,1,0:T(1,128)} custom-call(s32[32]{0:T(128)} %ids_far.1, s32[32]{0:T(128)} %counts_far.1, f32[3,32,512]{2,1,0:T(8,128)} %bitcast.2, f32[3,32,512]{2,1,0:T(8,128)} %bitcast.3), custom_call_target="tpu_custom_call" | custom-call | tf_op jit(solution)/shard_map/bucket/pallas_call | solution.py:206
  2.9 19.5 %all_to_all.5.arrived_ref = f32[16,1,6400]{2,1,0:T(1,128)S(1)} all-to-all(f32[16,1,6400]{2,1,0:T(1,128)} %bucket.1), channel_id=1, replica_groups=mesh['snap'=2,'gx'=16] {'gx'}, dimensions={0} | all-to-all | bytes 819200 | tf_op jit(solution)/shard_map/all_to_all | solution.py:637
  22.4 9.5 %deposit.1 = (bf16[4,544,512]{2,1,0:T(8,128)(2,1)S(1)}, f32[4,128,128]{2,1,0:T(8,128)S(1)}, f32[4,32,128]{2,1,0:T(8,128)S(1)}, f32[1056,128]{1,0:T(8,128)S(1)}, f32[704,128]{1,0:T(8,128)S(1)}) custom-call(f32[16,1,6400]{2,1,0:T(1,128)S(1)} %all_to_all.5.arrived_ref, bf16[18432,512]{1,0:T(8,128)(2,1)} %constant.2.clone.filter_far), custom_call_target="tpu_custom_call" | custom-call | tf_op jit(solution)/shard_map/deposit/pallas_call | solution.py:522
  32.0 0.3 collective-permute-start
  32.3 0.3 collective-permute-start.1
  32.5 4.0 %fine.1 = (f32[4,16,32,256]{3,2,1,0:T(8,128)}, f32[4,5,32,256]{3,2,1,0:T(8,128)S(1)}) custom-call(bf16[4,544,512]{2,1,0:T(8,128)(2,1)S(1)} %get-tuple-element.10.spread_ref, bf16[18432,512]{1,0:T(8,128)(2,1)} %constant.2.clone.filter_far), custom_call_target="tpu_custom_call" | custom-call | flops 570425344 | bytes 10000000 | tf_op jit(solution)/shard_map/fine/pallas_call | solution.py:493
  36.6 8.4 %collective-permute-done.1.high_ref = f32[704,128]{1,0:T(8,128)S(1)} collective-permute-done((f32[704,128]{1,0:T(8,128)S(1)}, f32[704,128]{1,0:T(8,128)S(1)}, u32[]{:S(2)}, u32[]{:S(2)}) %collective-permute-start.1) | collective-permute-done | bytes 360480 | tf_op jit(solution)/shard_map/ppermute | solution.py:640
  44.9 0.0 collective-permute-done.low_ref
  44.9 1.6 %join.1 = (f32[4,16,32,256]{3,2,1,0:T(8,128)}, f32[4,8,2048]{2,1,0:T(8,128)}, f32[4,4,512]{2,1,0:T(4,128)}) custom-call(f32[4,16,32,256]{3,2,1,0:T(8,128)} %get-tuple-element.11.inside_ref, f32[4,5,32,256]{3,2,1,0:T(8,128)S(1)} %get-tuple-element.12.rim_ref, f32[4,128,128]{2,1,0:T(8,128)S(1)} %get-tuple-element.13.mid_in_ref, ...), custom_call_target="tpu_custom_call", output_to_operand_aliasing={{0}: (0, {})} | custom-call | tf_op jit(solution)/shard_map/join/pallas_call | solution.py:609
Async XLA Ops:
  32.0 12.9 %collective-permute-start = (f32[1056,128]{1,0:T(8,128)S(1)}, f32[1056,128]{1,0:T(8,128)S(1)}, u32[]{:S(2)}, u32[]{:S(2)}) collective-permute-start(f32[1056,128]{1,0:T(8,128)S(1)} %get-tuple-element.15), channel_id=1, source_target_pairs={{0,1},{1,2},{2,3},{3,4},{4,5},{5,6},{6,7},{7,8},{8,9},{9,10},{10,1... | collective-permute-start | bytes 1622024 | tf_op jit(solution)/shard_map/ppermute | solution.py:639
  32.3 12.6 %collective-permute-start.1 = (f32[704,128]{1,0:T(8,128)S(1)}, f32[704,128]{1,0:T(8,128)S(1)}, u32[]{:S(2)}, u32[]{:S(2)}) collective-permute-start(f32[704,128]{1,0:T(8,128)S(1)} %get-tuple-element.16), channel_id=1, source_target_pairs={{0,15},{1,0},{2,1},{3,2},{4,3},{5,4},{6,5},{7,6},{8,7},{9,8},{10,9... | collective-permute-start | bytes 1081352 | tf_op jit(solution)/shard_map/ppermute | solution.py:640

commit v5 on v4

--- a/solution.py
+++ b/solution.py
@@ -550,26 +550,8 @@
 
 def join_kernel(
     inside_ref, rim_ref, mid_in_ref, coarse_in_ref, low_ref, high_ref,
-    fine_ref, mid_ref, coarse_ref, edge_ref, mid_sum, coarse_sum, sems,
+    fine_ref, mid_far, coarse_far, edge_ref, mid_ref, coarse_ref, mid_sum, coarse_sum, sems,
 ):
-    for c in range(4):
-        for plane in range(RIGHT):
-            row = (c * RIGHT + plane) * 2 * NY
-            edge_ref[c, plane, :, :LANES] = rim_ref[c, plane, :, :LANES] + low_ref[row : row + NY]
-            edge_ref[c, plane, :, LANES:] = (
-                rim_ref[c, plane, :, LANES:] + low_ref[row + NY : row + 2 * NY]
-            )
-        for plane in range(LEFT):
-            row = (c * LEFT + plane) * 2 * NY
-            at = RIGHT + plane
-            edge_ref[c, at, :, :LANES] = rim_ref[c, at, :, :LANES] + high_ref[row : row + NY]
-            edge_ref[c, at, :, LANES:] = (
-                rim_ref[c, at, :, LANES:] + high_ref[row + NY : row + 2 * NY]
-            )
-    first = pltpu.make_async_copy(edge_ref.at[:, :RIGHT], fine_ref.at[:, :RIGHT], sems.at[1])
-    last = pltpu.make_async_copy(edge_ref.at[:, RIGHT:], fine_ref.at[:, TILE - LEFT :], sems.at[0])
-    first.start()
-    last.start()
     mid_sum[...] = mid_in_ref[...]
     coarse_sum[...] = coarse_in_ref[...]
     for sent, planes, first_of in ((low_ref, RIGHT, False), (high_ref, LEFT, True)):
@@ -598,8 +580,32 @@
             coarse_ref[c, :, pair * LANES : (pair + 1) * LANES] = jnp.where(
                 lane < LANES // 2, even, odd
             )
+    mid_out = pltpu.make_async_copy(mid_ref, mid_far, sems.at[2])
+    coarse_out = pltpu.make_async_copy(coarse_ref, coarse_far, sems.at[3])
+    mid_out.start()
+    coarse_out.start()
+    for c in range(4):
+        for plane in range(RIGHT):
+            row = (c * RIGHT + plane) * 2 * NY
+            edge_ref[c, plane, :, :LANES] = rim_ref[c, plane, :, :LANES] + low_ref[row : row + NY]
+            edge_ref[c, plane, :, LANES:] = (
+                rim_ref[c, plane, :, LANES:] + low_ref[row + NY : row + 2 * NY]
+            )
+        for plane in range(LEFT):
+            row = (c * LEFT + plane) * 2 * NY
+            at = RIGHT + plane
+            edge_ref[c, at, :, :LANES] = rim_ref[c, at, :, :LANES] + high_ref[row : row + NY]
+            edge_ref[c, at, :, LANES:] = (
+                rim_ref[c, at, :, LANES:] + high_ref[row + NY : row + 2 * NY]
+            )
+    first = pltpu.make_async_copy(edge_ref.at[:, :RIGHT], fine_ref.at[:, :RIGHT], sems.at[1])
+    last = pltpu.make_async_copy(edge_ref.at[:, RIGHT:], fine_ref.at[:, TILE - LEFT :], sems.at[0])
+    first.start()
+    last.start()
     first.wait()
     last.wait()
+    mid_out.wait()
+    coarse_out.wait()
 
 
 def join(inside, rim, mid, coarse, from_low, from_high):
@@ -614,12 +620,14 @@
             jax.ShapeDtypeStruct((4, TILE // 4, NY // 4 * (NZ // 4)), f32),
         ],
         in_specs=[far] + [vmem] * 5,
-        out_specs=[far, vmem, vmem],
+        out_specs=[far] * 3,
         scratch_shapes=[
             pltpu.VMEM((4, RIGHT + LEFT, NY, NZ), f32),
+            pltpu.VMEM((4, TILE // 2, NY // 2 * (NZ // 2)), f32),
+            pltpu.VMEM((4, TILE // 4, NY // 4 * (NZ // 4)), f32),
             pltpu.VMEM(mid.shape, f32),
             pltpu.VMEM(coarse.shape, f32),
-            pltpu.SemaphoreType.DMA((2,)),
+            pltpu.SemaphoreType.DMA((4,)),
         ],
         input_output_aliases={0: 0},
         compiler_params=pltpu.CompilerParams(vmem_limit_bytes=10 * 2**20),

time: 46.8 us -> 46.3 us (0.989)
  Pallas kernels: 17.5 us -> 16.9 us
    pallas_call x1, Pallas kernels: 1.62 us -> 1.07 us  [join(): pl.pallas_call(join_kernel, out_shape=[jax.ShapeDtypeStruct((4, TILE, NY,...]
where the time goes in v5:
time: 46.3 us; the launch traced here: 46 us
  blocking collectives  19.5 us (42%)
  Pallas kernels  16.9 us (37%)
  waiting for transfers between devices  8.37 us (18%)
  between operations  0.66 us (1%)
  starting transfers between devices  0.56 us (1%)
    all_to_all x1, blocking collectives, on_device(): lax.all_to_all(outgoing, 'gx', split_axis=0, concat_axis=0, tiled=True)  19.5 us
    pallas_call x1, Pallas kernels, deposit(): pl.pallas_call(functools.partial(deposit_kernel, per_peer, capacity // LA...  9.53 us
    ppermute x1, waiting for transfers between devices, on_device(): lax.ppermute(left, 'gx', [(i, (i - 1) % devices) for i in range(devices)])  8.37 us
    pallas_call x1, Pallas kernels, fine(): pl.pallas_call(fine_kernel, out_shape=[jax.ShapeDtypeStruct((4, TILE, NY,...  4.01 us
    pallas_call x1, Pallas kernels, bucket(): pl.pallas_call(functools.partial(bucket_kernel, per_peer), out_shape=jax....  2.3 us
    pallas_call x1, Pallas kernels, join(): pl.pallas_call(join_kernel, out_shape=[jax.ShapeDtypeStruct((4, TILE, NY,...  1.07 us
  transfers between devices with their start and end apart: 2, of which 1 were waited for; matrix products, arithmetic and copies ran while one was open for 0% of the time, Pallas kernels for 9%

profile of v5, /device:TPU:1, one launch (start us, length us, event | category | flops | bytes accessed | tf_op | source)
XLA Modules:
  0.0 46.0 jit_solution(10815995721802842013)
XLA Ops:
  0.6 2.3 %bucket.1 = f32[16,1,6400]{2,1,0:T(1,128)} custom-call(s32[32]{0:T(128)} %ids_far.1, s32[32]{0:T(128)} %counts_far.1, f32[3,32,512]{2,1,0:T(8,128)} %bitcast.2, f32[3,32,512]{2,1,0:T(8,128)} %bitcast.3), custom_call_target="tpu_custom_call" | custom-call | tf_op jit(solution)/shard_map/bucket/pallas_call | solution.py:206
  2.9 19.5 %all_to_all.5.arrived_ref = f32[16,1,6400]{2,1,0:T(1,128)S(1)} all-to-all(f32[16,1,6400]{2,1,0:T(1,128)} %bucket.1), channel_id=1, replica_groups=mesh['snap'=2,'gx'=16] {'gx'}, dimensions={0} | all-to-all | bytes 819200 | tf_op jit(solution)/shard_map/all_to_all | solution.py:645
  22.4 9.5 %deposit.1 = (bf16[4,544,512]{2,1,0:T(8,128)(2,1)S(1)}, f32[4,128,128]{2,1,0:T(8,128)S(1)}, f32[4,32,128]{2,1,0:T(8,128)S(1)}, f32[1056,128]{1,0:T(8,128)S(1)}, f32[704,128]{1,0:T(8,128)S(1)}) custom-call(f32[16,1,6400]{2,1,0:T(1,128)S(1)} %all_to_all.5.arrived_ref, bf16[18432,512]{1,0:T(8,128)(2,1)} %constant.2.clone.filter_far), custom_call_target="tpu_custom_call" | custom-call | tf_op jit(solution)/shard_map/deposit/pallas_call | solution.py:522
  32.0 0.3 collective-permute-start
  32.3 0.3 collective-permute-start.1
  32.5 4.0 %fine.1 = (f32[4,16,32,256]{3,2,1,0:T(8,128)}, f32[4,5,32,256]{3,2,1,0:T(8,128)S(1)}) custom-call(bf16[4,544,512]{2,1,0:T(8,128)(2,1)S(1)} %get-tuple-element.10.spread_ref, bf16[18432,512]{1,0:T(8,128)(2,1)} %constant.2.clone.filter_far), custom_call_target="tpu_custom_call" | custom-call | flops 570425344 | bytes 10000000 | tf_op jit(solution)/shard_map/fine/pallas_call | solution.py:493
  36.5 8.4 %collective-permute-done.1.high_ref = f32[704,128]{1,0:T(8,128)S(1)} collective-permute-done((f32[704,128]{1,0:T(8,128)S(1)}, f32[704,128]{1,0:T(8,128)S(1)}, u32[]{:S(2)}, u32[]{:S(2)}) %collective-permute-start.1) | collective-permute-done | bytes 360480 | tf_op jit(solution)/shard_map/ppermute | solution.py:648
  44.9 0.0 collective-permute-done.low_ref
  44.9 1.1 %join.1 = (f32[4,16,32,256]{3,2,1,0:T(8,128)}, f32[4,8,2048]{2,1,0:T(8,128)}, f32[4,4,512]{2,1,0:T(4,128)}) custom-call(f32[4,16,32,256]{3,2,1,0:T(8,128)} %get-tuple-element.11.inside_ref, f32[4,5,32,256]{3,2,1,0:T(8,128)S(1)} %get-tuple-element.12.rim_ref, f32[4,128,128]{2,1,0:T(8,128)S(1)} %get-tuple-element.13.mid_in_ref, ...), custom_call_target="tpu_custom_call", output_to_operand_aliasing={{0}: (0, {})} | custom-call | tf_op jit(solution)/shard_map/join/pallas_call | solution.py:615
Async XLA Ops:
  32.0 12.9 %collective-permute-start = (f32[1056,128]{1,0:T(8,128)S(1)}, f32[1056,128]{1,0:T(8,128)S(1)}, u32[]{:S(2)}, u32[]{:S(2)}) collective-permute-start(f32[1056,128]{1,0:T(8,128)S(1)} %get-tuple-element.15), channel_id=1, source_target_pairs={{0,1},{1,2},{2,3},{3,4},{4,5},{5,6},{6,7},{7,8},{8,9},{9,10},{10,1... | collective-permute-start | bytes 1622024 | tf_op jit(solution)/shard_map/ppermute | solution.py:647
  32.3 12.6 %collective-permute-start.1 = (f32[704,128]{1,0:T(8,128)S(1)}, f32[704,128]{1,0:T(8,128)S(1)}, u32[]{:S(2)}, u32[]{:S(2)}) collective-permute-start(f32[704,128]{1,0:T(8,128)S(1)} %get-tuple-element.16), channel_id=1, source_target_pairs={{0,15},{1,0},{2,1},{3,2},{4,3},{5,4},{6,5},{7,6},{8,7},{9,8},{10,9... | collective-permute-start | bytes 1081352 | tf_op jit(solution)/shard_map/ppermute | solution.py:648
